TPU v7x, 256 devices: a whole 4x4x8 slice. The times are simulated.
256 devices in a mesh: row: 64 (over x, z, core), col: 4 (over y).
Axes of the slice: x: 4, y: 4, z: 8, core: 2. Of those that a mesh axis runs over, the one named last changes fastest.
Arguments:
- features: bfloat16 [262144, 512], P('row'), may hold values from -6 to 6
- history: bfloat16 [262144, 512], P('row'), may hold values from 0 to 2
- weight_one: bfloat16 [512, 512], P(None, 'col'), may hold values from -0.25 to 0.25
- weight_two: bfloat16 [512, 512], P(None, 'col'), may hold values from -0.25 to 0.25
- bias_one: float32 [512], P('col'), may hold values from -3 to 3
- bias_two: float32 [512], P('col'), may hold values from -3 to 3
- adjacency: bfloat16 [12288, 128, 128], P('row'), may hold values from 0 to 0.071777344
- halo_owner: int32 [64, 96], P('row'), may hold values from -1 to 63, as said below
- halo_block: int32 [64, 96], P('row'), may hold values from 0 to 31, as said below
- tile_target: int32 [64, 192], P('row'), may hold values from 0 to 31
- tile_source: int32 [64, 192], P('row'), may hold values from 0 to 127, as said below
- tile_count: int32 [64], P('row'), may hold values from 80 to 192, as said below
Outputs:
- hidden: bfloat16 [262144, 512], P('row', 'col')
- embedding: bfloat16 [262144, 512], P('row', 'col')
Inputs may be any that keep to these rules, and one draw needn't show every extreme that they name: `halo_owner`: used slots come first and are followed only by unused ones (-1); at least half of the 96 slots are used and some partition uses all; no partition names itself; at most 2 used slots of one partition name the same owner, and some partition reaches 2. `halo_block`: used slots of one partition that name the same owner name different blocks. `tile_source`: live tiles name only local blocks or used halo slots. `tile_count`: some partition has all 192 tiles live.
All inputs are finite; a program needn't handle non-finite values.
Results may differ from a plain program's by a relative error of at most 0.0046.
Values may be sent and summed in bfloat16 or wider, within the bound.
A program may use at most 128 MiB of HBM per device.

v0:
```python
import jax
import jax.numpy as jnp
from jax import lax
from jax.sharding import PartitionSpec as P

BLOCK = 128
CAP = 2
NB = 32


def aggregate(own_blocks, halo_blocks, adjacency, targets, source_ids, live_count):
    sources = jnp.concatenate([own_blocks, halo_blocks], axis=0)
    picked = sources[source_ids]
    products = jnp.einsum("tab,tbw->taw", adjacency, picked, preferred_element_type=jnp.float32)
    live_tiles = jnp.arange(targets.shape[0], dtype=jnp.int32) < live_count
    scatter_map = (
        (targets[None, :] == jnp.arange(NB, dtype=jnp.int32)[:, None]) & live_tiles[None, :]
    ).astype(jnp.float32)
    return jnp.einsum("nt,taw->naw", scatter_map, products, precision=lax.Precision.HIGHEST)


def local(
    features,
    history,
    weight_one,
    weight_two,
    bias_one,
    bias_two,
    adjacency,
    halo_owner,
    halo_block,
    tile_target,
    tile_source,
    tile_count,
):
    part_count = lax.axis_size("row")
    col_width = weight_one.shape[1]
    owners = halo_owner[0]
    wanted_blocks = halo_block[0]
    in_use = owners >= 0
    slot_ids = jnp.arange(owners.shape[0], dtype=jnp.int32)
    earlier = (
        (owners[:, None] == owners[None, :])
        & (slot_ids[None, :] < slot_ids[:, None])
        & in_use[None, :]
    )
    position = jnp.sum(earlier.astype(jnp.int32), axis=1)
    matches = (
        (owners[None, None, :] == jnp.arange(part_count, dtype=jnp.int32)[:, None, None])
        & (position[None, None, :] == jnp.arange(CAP, dtype=jnp.int32)[None, :, None])
        & in_use[None, None, :]
    )
    wanted = jnp.sum(jnp.where(matches, wanted_blocks[None, None, :] + 1, 0), axis=2) - 1
    requested = lax.all_to_all(wanted, "row", split_axis=0, concat_axis=0, tiled=True)
    pick_index = jnp.clip(requested, 0, NB - 1)
    arrival = jnp.where(in_use, owners, 0) * CAP + position
    targets = tile_target[0]
    source_ids = tile_source[0]
    live_count = tile_count[0]
    proj_one = (
        jnp.dot(features, weight_one, preferred_element_type=jnp.float32)
        .astype(jnp.bfloat16)
        .reshape(NB, BLOCK, col_width)
    )
    proj_past = (
        jnp.dot(history, weight_two, preferred_element_type=jnp.float32)
        .astype(jnp.bfloat16)
        .reshape(NB, BLOCK, col_width)
    )
    came_one = lax.all_to_all(proj_one[pick_index], "row", split_axis=0, concat_axis=0, tiled=True)
    halo_one = came_one.reshape(-1, BLOCK, col_width)[arrival]
    summed_one = aggregate(proj_one, halo_one, adjacency, targets, source_ids, live_count)
    hidden = (
        jnp.maximum(summed_one + bias_one, 0.0).astype(jnp.bfloat16).reshape(NB * BLOCK, col_width)
    )
    full_weight = lax.all_gather(weight_two, "col", axis=1, tiled=True)
    own_rows = lax.dynamic_slice_in_dim(
        full_weight, lax.axis_index("col") * col_width, col_width, 0
    )
    partial_value = jnp.dot(hidden, own_rows, preferred_element_type=jnp.float32)
    proj_two = lax.psum_scatter(
        partial_value.astype(jnp.bfloat16), "col", scatter_dimension=1, tiled=True
    )
    came_two = lax.all_to_all(proj_past[pick_index], "row", split_axis=0, concat_axis=0, tiled=True)
    halo_two = came_two.reshape(-1, BLOCK, col_width)[arrival]
    summed_two = aggregate(
        proj_two.reshape(NB, BLOCK, col_width), halo_two, adjacency, targets, source_ids, live_count
    )
    embedding = (summed_two + bias_two).astype(jnp.bfloat16).reshape(NB * BLOCK, col_width)
    return (hidden, embedding)


def solution(mesh):
    return jax.shard_map(
        local,
        mesh=mesh,
        in_specs=(
            P("row", None),
            P("row", None),
            P(None, "col"),
            P(None, "col"),
            P("col"),
            P("col"),
            P("row", None, None),
            P("row", None),
            P("row", None),
            P("row", None),
            P("row", None),
            P("row"),
        ),
        out_specs=(P("row", "col"), P("row", "col")),
        check_vma=False,
    )
```

profile of v0, /device:TPU:1, one launch (start us, length us, event | category | flops | bytes accessed | tf_op | source)
XLA Modules:
  0.0 377.9 jit_solution(444298443836190601)
XLA Ops:
  7.2 0.7 compare_bitcast_fusion
  8.5 0.7 iota_compare_fusion.1
  9.2 0.9 convert_reduce_fusion
  10.1 0.7 add_bitcast_fusion.1
  10.9 0.7 copy.43
  11.6 13.0 %all-to-all-start = ((s32[64,1,2]{2,1,0:T(1,128)}), s32[64,1,2]{2,1,0:T(1,128)S(1)}, u32[]{:S(2)}, u32[]{:S(2)}) async-start(s32[64,1,2]{2,1,0:T(1,128)} %copy.43), calls=%async_computation | async-start | bytes 65536 | tf_op jit(solution)/shard_map/all_to_all | solution.py:54
  24.6 3.4 convolution_convert_fusion.2
  28.1 5.8 %all-to-all-done = s32[64,1,2]{2,1,0:T(1,128)S(1)} async-done(((s32[64,1,2]{2,1,0:T(1,128)}), s32[64,1,2]{2,1,0:T(1,128)S(1)}, u32[]{:S(2)}, u32[]{:S(2)}) %all-to-all-start) | async-done | bytes 544 | tf_op jit(solution)/shard_map/all_to_all | solution.py:54
  34.2 3.1 gather_fusion
  37.3 5.8 %all-to-all-start.1 = ((bf16[64,2,128,128]{3,2,1,0:T(8,128)(2,1)}), bf16[64,2,128,128]{3,2,1,0:T(8,128)(2,1)}, u32[]{:S(2)}, u32[]{:S(2)}) async-start(bf16[64,2,128,128]{3,2,1,0:T(8,128)(2,1)} %bitcast.61), calls=%async_computation.1 | async-start | bytes 8388608 | tf_op jit(solution)/shard_map/all_to_all | solution.py:70
  43.9 12.6 %all_gather.3 = bf16[512,512]{1,0:T(8,128)(2,1)S(1)} all-gather(bf16[512,128]{1,0:T(8,128)(2,1)S(1)} %copy-done.3), channel_id=1, replica_groups=mesh['row'=64,'col'=4] {'col'}, dimensions={1}, use_global_device_ids=true | all-gather | bytes 655360 | tf_op jit(solution)/shard_map/all_gather | solution.py:76
  56.5 82.6 %all-to-all-done.1 = bf16[64,2,128,128]{3,2,1,0:T(8,128)(2,1)} async-done(((bf16[64,2,128,128]{3,2,1,0:T(8,128)(2,1)}), bf16[64,2,128,128]{3,2,1,0:T(8,128)(2,1)}, u32[]{:S(2)}, u32[]{:S(2)}) %all-to-all-start.1) | async-done | bytes 4194336 | tf_op jit(solution)/shard_map/all_to_all | solution.py:70
  139.0 4.9 %gather_fusion.1 = bf16[96,128,128]{2,1,0:T(8,128)(2,1)} fusion(bf16[128,128,128]{2,1,0:T(8,128)(2,1)} %bitcast.10, s32[1024]{0:T(1024)S(1)} %pad_clamp_fusion.1), kind=kCustom, calls=%fused_computation.1 | custom fusion | bytes 6291840 | tf_op jit(solution)/shard_map/gather | solution.py:71
  143.9 4.2 %pad_maximum_fusion = bf16[128,128,128]{2,1,0:T(8,128)(2,1)} fusion(bf16[96,128,128]{2,1,0:T(8,128)(2,1)} %gather_fusion.1, bf16[32,128,128]{2,1,0:T(8,128)(2,1)S(1)} %bitcast.59), kind=kLoop, calls=%fused_computation.11 | loop fusion | flops 2097152 | bytes 8388608 | tf_op jit(solution)/shard_map/concatenate | solution.py:12
  148.1 10.2 %gather_fusion.2 = bf16[192,128,128]{2,1,0:T(8,128)(2,1)} fusion(bf16[128,128,128]{2,1,0:T(8,128)(2,1)} %pad_maximum_fusion, s32[1024]{0:T(1024)S(1)} %pad_clamp_fusion), kind=kCustom, calls=%fused_computation.2 | custom fusion | bytes 12583680 | tf_op jit(solution)/shard_map/gather | solution.py:13
  158.3 13.7 %convolution_bitcast_fusion.1 = f32[192,128,128]{1,2,0:T(8,128)} fusion(bf16[192,128,128]{2,1,0:T(8,128)(2,1)} %gather_fusion.2, bf16[192,128,128]{2,1,0:T(8,128)(2,1)} %param.18), kind=kOutput, calls=%fused_computation.10 | convolution fusion | flops 805306368 | bytes 25165824 | tf_op jit(solution)/shard_map/tab,tbw->taw/dot_general | solution.py:14
  172.0 12.8 %copy.47 = f32[192,128,128]{2,0,1:T(8,128)} copy(f32[192,128,128]{1,2,0:T(8,128)} %convolution_bitcast_fusion.1) | data formatting | bytes 25165824 | tf_op jit(solution)/shard_map/tab,tbw->taw/dot_general | solution.py:14
  184.8 9.7 %maximum_convert_fusion = bf16[32,128,128]{2,0,1:T(8,128)(2,1)S(1)} fusion(f32[192,128,128]{2,0,1:T(8,128)} %copy.47, f32[128]{0:T(128)S(1)} %copy-done.7, s32[192]{0:T(256)S(1)} %bitcast.72, pred[192]{0:T(512)(128)(4,1)S(1)} %iota_compare_fusion.4), kind=kOutput, calls=%fused_computation.14 | convolution fusion | flops 1209544704 | bytes 13632960 | tf_op jit(solution)/shard_map/nt,taw->naw/dot_general | solution.py:19
  194.9 1.0 copy-done.2
  195.9 3.2 convolution_convert_fusion
  199.1 6.4 %copy.54 = bf16[4096,512]{0,1:T(8,128)(2,1)} copy(bf16[4096,512]{1,0:T(8,128)(2,1)} %convolution_convert_fusion) | data formatting | bytes 8388608
  205.5 3.4 convolution_convert_fusion.1
  209.0 3.1 gather_fusion.3
  212.1 102.1 %all_to_all.16 = bf16[64,2,128,128]{3,2,1,0:T(8,128)(2,1)} all-to-all(bf16[64,2,128,128]{3,2,1,0:T(8,128)(2,1)} %bitcast.63), channel_id=1, replica_groups=mesh['row'=64,'col'=4] {'row'}, dimensions={0} | all-to-all | bytes 8388608 | tf_op jit(solution)/shard_map/all_to_all | solution.py:84
  314.2 3.3 gather_fusion.4
  317.5 2.3 copy.55
  319.8 3.5 pad_maximum_fusion.1
  323.3 10.2 %gather_fusion.5 = bf16[192,128,128]{2,1,0:T(8,128)(2,1)} fusion(bf16[128,128,128]{2,1,0:T(8,128)(2,1)} %pad_maximum_fusion.1, s32[1024]{0:T(1024)S(1)} %pad_clamp_fusion), kind=kCustom, calls=%fused_computation.5 | custom fusion | bytes 12583680 | tf_op jit(solution)/shard_map/gather | solution.py:13
  333.5 13.7 %convolution_bitcast_fusion = f32[192,128,128]{1,2,0:T(8,128)} fusion(bf16[192,128,128]{2,1,0:T(8,128)(2,1)} %gather_fusion.5, bf16[192,128,128]{2,1,0:T(8,128)(2,1)} %param.18), kind=kOutput, calls=%fused_computation.9 | convolution fusion | flops 805306368 | bytes 25165824 | tf_op jit(solution)/shard_map/tab,tbw->taw/dot_general | solution.py:14
  347.2 12.8 %copy.50 = f32[192,128,128]{2,0,1:T(8,128)} copy(f32[192,128,128]{1,2,0:T(8,128)} %convolution_bitcast_fusion) | data formatting | bytes 25165824 | tf_op jit(solution)/shard_map/tab,tbw->taw/dot_general | solution.py:14
  359.9 9.7 %add_convert_fusion = bf16[32,128,128]{2,0,1:T(8,128)(2,1)S(1)} fusion(f32[192,128,128]{2,0,1:T(8,128)} %copy.50, f32[128]{0:T(128)S(1)} %copy-done.8, s32[192]{0:T(256)S(1)} %bitcast.73, pred[192]{0:T(512)(128)(4,1)S(1)} %iota_compare_fusion.4), kind=kOutput, calls=%fused_computation.13 | convolution fusion | flops 1209020416 | bytes 13632960 | tf_op jit(solution)/shard_map/nt,taw->naw/dot_general | solution.py:19
  369.6 1.4 copy.51
  (35 shorter events, 1.7 us)
Async XLA Ops:
  7.2 17.5 %copy-start = (bf16[512,128]{1,0:T(8,128)(2,1)S(1)}, bf16[512,128]{1,0:T(8,128)(2,1)}, u32[]{:S(2)}) copy-start(bf16[512,128]{1,0:T(8,128)(2,1)} %param.14) | copy-start | bytes 393220
  11.6 22.2 %all-to-all-start = ((s32[64,1,2]{2,1,0:T(1,128)}), s32[64,1,2]{2,1,0:T(1,128)S(1)}, u32[]{:S(2)}, u32[]{:S(2)}) async-start(s32[64,1,2]{2,1,0:T(1,128)} %copy.43), calls=%async_computation | async-start | bytes 65536 | tf_op jit(solution)/shard_map/all_to_all | solution.py:54
  37.3 6.5 %copy-start.4 = (s32[1,96]{1,0:T(1,128)S(1)}, s32[1,96]{1,0:T(1,128)}, u32[]{:S(2)}) copy-start(s32[1,96]{1,0:T(1,128)} %param.19) | copy-start | bytes 1156
  37.3 6.6 %copy-start.6 = (s32[1,192]{1,0:T(1,128)S(1)}, s32[1,192]{1,0:T(1,128)}, u32[]{:S(2)}) copy-start(s32[1,192]{1,0:T(1,128)} %param.22) | copy-start | bytes 2308
  37.3 6.6 %copy-start.3 = (bf16[512,128]{1,0:T(8,128)(2,1)S(1)}, bf16[512,128]{1,0:T(8,128)(2,1)}, u32[]{:S(2)}) copy-start(bf16[512,128]{1,0:T(8,128)(2,1)} %param.15) | copy-start | bytes 393220
  37.3 101.8 %all-to-all-start.1 = ((bf16[64,2,128,128]{3,2,1,0:T(8,128)(2,1)}), bf16[64,2,128,128]{3,2,1,0:T(8,128)(2,1)}, u32[]{:S(2)}, u32[]{:S(2)}) async-start(bf16[64,2,128,128]{3,2,1,0:T(8,128)(2,1)} %bitcast.61), calls=%async_computation.1 | async-start | bytes 8388608 | tf_op jit(solution)/shard_map/all_to_all | solution.py:70
  43.1 274.4 %reduce-scatter.4.cloned.1.call-start = ((), (), s32[]{:S(2)}) async-start(), calls=%async_computation.4 | async-start | bytes 5242880
  172.0 12.8 %copy-start.5 = (s32[1,192]{1,0:T(1,128)S(1)}, s32[1,192]{1,0:T(1,128)}, u32[]{:S(2)}) copy-start(s32[1,192]{1,0:T(1,128)} %param.21) | copy-start | bytes 2308
  172.0 12.8 %copy-start.7 = (f32[128]{0:T(128)S(1)}, f32[128]{0:T(128)}, u32[]{:S(2)}) copy-start(f32[128]{0:T(128)} %param.16) | copy-start | bytes 1540
  194.9 1.0 copy-start.2
  347.2 12.8 %copy-start.8 = (f32[128]{0:T(128)S(1)}, f32[128]{0:T(128)}, u32[]{:S(2)}) copy-start(f32[128]{0:T(128)} %param.17) | copy-start | bytes 1540
  359.9 11.1 %copy-start.1 = (bf16[512,128]{1,0:T(8,128)(2,1)S(1)}, bf16[512,128]{1,0:T(8,128)(2,1)}, u32[]{:S(2)}) copy-start(bf16[512,128]{1,0:T(8,128)(2,1)} %param.14) | copy-start | bytes 393220
Sparse Core Ops, SparseCore 0:
  205.7 46.0 reduce-scatter.3
where the time goes:
time: 379 us; the launch traced here: 378 us
  blocking collectives  115 us (30%)
  waiting for transfers between devices  88.4 us (23%)
  local copies, waits for them, and re-layouts  72.8 us (19%)
  matrix products  56.8 us (15%)
  starting transfers between devices  18.8 us (5%)
  between operations  14.9 us (4%)
  other arithmetic  11.5 us (3%)
    all_to_all x1, blocking collectives, local(): lax.all_to_all(proj_past[pick_index], 'row', split_axis=0, concat_axis=0,...  102 us
    all_to_all x1, waiting for transfers between devices, local(): lax.all_to_all(proj_one[pick_index], 'row', split_axis=0, concat_axis=0,...  82.6 us
    dot_general x2, matrix products, aggregate(): jnp.einsum('tab,tbw->taw', adjacency, picked, preferred_element_type=jnp....  27.3 us
    dot_general x2, local copies, waits for them, and re-layouts, aggregate(): jnp.einsum('tab,tbw->taw', adjacency, picked, preferred_element_type=jnp....  25.5 us
    gather x2, local copies, waits for them, and re-layouts, aggregate(): picked = sources[source_ids]  20.4 us
    dot_general x2, matrix products, aggregate(): jnp.einsum('nt,taw->naw', scatter_map, products, precision=lax.Precision....  19.4 us
    all_to_all x1, starting transfers between devices, local(): lax.all_to_all(wanted, 'row', split_axis=0, concat_axis=0, tiled=True)  13 us
    all_gather x1, blocking collectives, local(): full_weight = lax.all_gather(weight_two, 'col', axis=1, tiled=True)  12.6 us
  transfers between devices with their start and end apart: 3, of which 2 were waited for; matrix products, arithmetic and copies ran while one was open for 4% of the time, Pallas kernels for 0%

commit v1 on v0

v1 whole, which is shorter than its diff:
```python
import functools

import jax
import jax.numpy as jnp
from jax import lax
from jax.experimental import pallas as pl
from jax.experimental.pallas import tpu as pltpu
from jax.sharding import PartitionSpec as P

BLOCK = 128
NB = 32
TILES = 192
HALO = 96
NX, NZ, NY = 4, 8, 4
GROUPS = 8
SHARE = 16
UNROLL = 8
LIST = TILES + UNROLL
CHUNKS = 4
PER = GROUPS // CHUNKS
MESH = pl.DeviceIdType.MESH

STEPS = (0, 7, 1, 6, 2, 5, 3, 4)

SMEM = pl.BlockSpec(memory_space=pltpu.SMEM)
VMEM = pl.BlockSpec(memory_space=pltpu.VMEM)
ANY = pl.BlockSpec(memory_space=pl.ANY)
PARAMS = pltpu.CompilerParams(vmem_limit_bytes=40 * 2**20)


def row_of(x, z, k):
    return x * (NZ * 2) + z * 2 + k


def member(x, k, group):
    dx, dk = group // 2, group % 2
    return lax.rem(x + dx, NX), k + dk - 2 * k * dk


def prepare_kernel(ids, owner, block, wanted, place):
    x, z, k = ids[0], ids[1], ids[2]

    @pl.loop(0, 128, unroll=8)
    def _(i):
        wanted[0, i] = 0
        place[0, i] = 0

    @pl.loop(0, 64, unroll=8)
    def _(i):
        wanted[1, i] = 0

    @pl.loop(0, HALO)
    def _(h):
        named = owner[0, h]
        o = jnp.maximum(named, 0)
        live = named >= 0
        nth = jnp.where(live, wanted[1, o], 0)
        wanted[1, o] = jnp.where(live, nth + 1, wanted[1, o])
        at = 2 * o + nth
        wanted[0, at] = jnp.where(live, block[0, h], wanted[0, at])
        ox, oz, ok = o // 16, (o // 2) % 8, o % 2
        group = lax.rem(x - ox + NX, NX) * 2 + (k + ok - 2 * k * ok)
        step = lax.rem(oz - z + NZ, NZ)
        spot = jnp.int32(0)
        for i, s in enumerate(STEPS):
            spot = jnp.where(step == s, 2 * i, spot)
        place[0, h] = group * SHARE + spot + nth


def prepare(ids, owner, block):
    return pl.pallas_call(
        prepare_kernel,
        out_shape=(
            jax.ShapeDtypeStruct((8, 128), jnp.int32),
            jax.ShapeDtypeStruct((1, 128), jnp.int32),
        ),
        in_specs=[SMEM] * 3,
        out_specs=(SMEM, SMEM),
        cost_estimate=pl.CostEstimate(flops=0, bytes_accessed=16 << 20, transcendentals=0),
        name="prepare",
    )(ids, owner, block)


def sort_kernel(target, source, count, place, lists, counts, order, keep):
    @pl.loop(0, LIST, unroll=8)
    def _(i):
        for c in range(2):
            lists[c, i] = NB << 16

    @pl.loop(0, TILES, unroll=8)
    def _(i):
        order[0, i] = 0
        keep[0, i] = 0.0

    @pl.loop(0, NB, unroll=8)
    def _(i):
        order[1, i] = 0
        order[2, i] = 0

    counts[0, 0] = 0
    live = count[0]
    counts[0, 1] = live

    @pl.loop(0, live)
    def _(t):
        s = source[0, t]
        b = target[0, t]
        own = s < NB
        spot = jnp.where(own, s, NB + place[0, jnp.clip(s - NB, 0, HALO - 1)])
        entry = t | (spot << 8) | (b << 16)
        lists[1, t] = entry
        n = counts[0, 0]
        lists[0, n] = entry
        counts[0, 0] = n + jnp.where(own, 1, 0)
        order[1, b] = order[1, b] + jnp.where(own, 0, 1)

    n = counts[0, 0]
    lists[0, n] = NB << 16

    def start(b, at):
        many = order[1, b]
        order[2, b] = at
        order[1, b] = jnp.maximum(at + many - 1, 0)
        keep[1, b] = jnp.where(many > 0, 1.0, 0.0)
        return at + many

    lax.fori_loop(0, NB, start, jnp.int32(0))

    @pl.loop(0, NB)
    def _(b):
        order[3, b] = order[2, b]

    @pl.loop(0, live)
    def _(t):
        e = lists[1, t]
        b = e >> 16
        spot = (e >> 8) & 255

        @pl.when(spot >= NB)
        def _():
            at = order[2, b]
            order[0, at] = (e & 255) | ((spot - NB) << 8)
            keep[0, at] = jnp.where(at == order[3, b], 0.0, 1.0)
            order[2, b] = at + 1


def sort_tiles(target, source, count, place):
    return pl.pallas_call(
        sort_kernel,
        out_shape=(
            jax.ShapeDtypeStruct((2, LIST), jnp.int32),
            jax.ShapeDtypeStruct((1, 2), jnp.int32),
            jax.ShapeDtypeStruct((4, TILES), jnp.int32),
            jax.ShapeDtypeStruct((2, TILES), jnp.float32),
        ),
        in_specs=[SMEM] * 4,
        out_specs=(SMEM,) * 4,
        cost_estimate=pl.CostEstimate(flops=0, bytes_accessed=24 << 20, transcendentals=0),
        name="sort_tiles",
    )(target, source, count, place)


def gather_kernel(kind, widths, last, *refs):
    lists, counts, adjacency = refs[:3]
    pieces = refs[3 : 3 + len(widths)]
    rest = refs[3 + len(widths) :]
    if last:
        bias, rest = rest[0], rest[1:]
    out, total, held, sem = rest
    copies, at = [], 0
    for i, (piece, width) in enumerate(zip(pieces, widths)):
        copies.append(
            pltpu.make_async_copy(piece, held.at[pl.ds(at, width)], sem.at[i])
        )
        at += width
    for copy in copies:
        copy.start()
    total[...] = jnp.zeros_like(total)
    for copy in copies:
        copy.wait()

    @pl.loop(0, (counts[0, kind] + UNROLL - 1) // UNROLL)
    def _(step):
        entries = [lists[kind, step * UNROLL + i] for i in range(UNROLL)]
        products = [
            jnp.dot(
                adjacency[e & 255],
                held[(e >> 8) & 255],
                preferred_element_type=jnp.float32,
            )
            for e in entries
        ]
        for e, product in zip(entries, products):
            total[e >> 16] += product

    if last:

        @pl.loop(0, NB, unroll=2)
        def _(b):
            out[b] = (total[b] + bias[...]).astype(jnp.bfloat16)
    else:
        out[...] = total[0:NB]


def gather(kind, lists, counts, adjacency, pieces, bias=None):
    last = bias is not None
    widths = [p.shape[0] for p in pieces]
    args = [lists, counts, adjacency, *pieces]
    specs = [SMEM, SMEM, VMEM] + [ANY] * len(pieces)
    if last:
        args.append(bias.reshape(1, BLOCK))
        specs.append(VMEM)
    return pl.pallas_call(
        functools.partial(gather_kernel, kind, widths, last),
        out_shape=jax.ShapeDtypeStruct(
            (NB, BLOCK, BLOCK), jnp.bfloat16 if last else jnp.float32
        ),
        in_specs=specs,
        out_specs=VMEM,
        scratch_shapes=[
            pltpu.VMEM((NB + 1, BLOCK, BLOCK), jnp.float32),
            pltpu.VMEM((sum(widths), BLOCK, BLOCK), jnp.bfloat16),
            pltpu.SemaphoreType.DMA((len(pieces),)),
        ],
        compiler_params=PARAMS,
        cost_estimate=pl.CostEstimate(
            flops=2 * 64 * BLOCK**3, bytes_accessed=16 << 20, transcendentals=0
        ),
        name=("own", "all")[kind] + "_tiles",
    )(*args)


COPIES = 112


def exchange_kernel(
    mine,
    order,
    keep,
    bias,
    weight,
    table_one,
    up_one,
    down_one,
    table_past,
    own,
    adjacency,
    hidden,
    table_two,
    halo_two,
    wanted_all,
    wanted,
    up_two,
    down_two,
    up_past,
    down_past,
    up_past_two,
    down_past_two,
    relay_out,
    relay_in,
    share,
    halo_one,
    sums,
    near_y,
    far_y,
    send_sem,
    recv_sem,
    local_sem,
):
    row = lax.axis_index("row")
    y = lax.axis_index("col")
    x, z, k = row // 16, lax.rem(row // 2, NZ), lax.rem(row, 2)
    me = x * 2 + k
    used = [0]

    def at_z(step):
        return (row_of(x, lax.rem(z + step + NZ, NZ), k), y)

    def at_slab(group):
        ox, ok = member(x, k, group)
        return (row_of(ox, z, ok), y)

    def at_y(step):
        return (row, lax.rem(y + step + NY, NY))

    peers = [at_z(s) for s in (1, -1, 2, -2)]
    peers += [at_slab(g) for g in range(1, GROUPS)]
    peers += [at_y(s) for s in (1, -1)]

    barrier = pltpu.get_barrier_semaphore()
    for peer in peers:
        pl.semaphore_signal(barrier, inc=1, device_id=peer, device_id_type=MESH)
    pl.semaphore_wait(barrier, len(peers))

    started = []

    def send(src, dst, device):
        i = used[0]
        used[0] += 1
        copy = pltpu.make_async_remote_copy(
            src_ref=src,
            dst_ref=dst,
            send_sem=send_sem.at[i],
            recv_sem=recv_sem.at[i],
            device_id=device,
            device_id_type=MESH,
        )
        copy.start()
        started.append(copy)
        return copy

    asks = [
        send(mine, wanted_all.at[2, me], at_slab(g)) for g in range(1, GROUPS)
    ]
    hop = [
        send(up_one, up_two, at_z(1)),
        send(down_one, down_two, at_z(-1)),
    ]
    wanted_all[2, me] = mine[...]
    for copy in asks:
        copy.wait_recv()
    asks = [
        send(wanted_all.at[2], wanted_all.at[2 - s], at_z(s)) for s in (1, -1, 2, -2)
    ]
    for copy in asks:
        copy.wait_recv()
    to_scalars = pltpu.make_async_copy(wanted_all, wanted, local_sem.at[0])
    to_scalars.start()
    to_scalars.wait()

    def pick(shift, group, step, slot):
        ox, ok = member(x, k, group)
        o = row_of(x, lax.rem(z + step + NZ, NZ), k)
        return wanted[2 + shift, ox * 2 + ok, 0, 2 * o + slot]

    def pack_share(parts):
        @pl.loop(0, GROUPS)
        def _(g):
            for i, table in parts:
                for slot in range(2):
                    share[g * SHARE + 2 * i + slot] = table[pick(0, g, STEPS[i], slot)]

    def send_share(layer, g, start, size, halo):
        place = pl.ds(g * SHARE + start, size)
        return send(share.at[place], halo.at[place], at_slab(g))

    def pack_relay(up, down):
        @pl.loop(0, GROUPS)
        def _(g):
            for side, (table, sign) in enumerate(((up, 1), (down, -1))):
                for slot in range(2):
                    relay_out[side, g * 2 + slot] = table[pick(sign, g, -2 * sign, slot)]
                relay_out[2 + side, g] = table[pick(2 * sign, g, -2 * sign, side)]

    def send_relay(layer, c):
        copies = []
        for side, sign in ((0, 1), (1, -1)):
            near = pl.ds(c * PER * 2, PER * 2)
            far = pl.ds(c * PER, PER)
            copies.append(
                send(relay_out.at[2 + side, far], relay_in.at[layer, 2 + side, far], at_z(2 * sign))
            )
            copies.append(
                send(relay_out.at[side, near], relay_in.at[layer, side, near], at_z(sign))
            )
        return copies

    def pack_far(layer, c):
        for g in range(c * PER, (c + 1) * PER):
            place = g * SHARE
            share[place + 10] = relay_in[layer, 0, 2 * g]
            share[place + 11] = relay_in[layer, 0, 2 * g + 1]
            share[place + 12] = relay_in[layer, 1, 2 * g]
            share[place + 13] = relay_in[layer, 1, 2 * g + 1]
            share[place + 14] = relay_in[layer, 2, g]
            share[place + 15] = relay_in[layer, 3, g]

    def forward_far(layer, relays, halo, between):
        copies = []
        for c in range(CHUNKS):
            for copy in relays[c]:
                copy.wait_recv()
            pack_far(layer, c)
            for g in range(max(1, c * PER), (c + 1) * PER):
                copies.append(send_share(layer, g, 10, 6, halo))
            if c in between:
                between[c]()
        return copies

    pack_share([(0, table_one), (1, up_one), (2, down_one)])
    halo_copies = [send_share(0, g, 0, 6, halo_one) for g in range(1, GROUPS)]
    for copy in hop:
        copy.wait_recv()
    pack_relay(up_two, down_two)
    relays = [send_relay(0, c) for c in range(CHUNKS)]
    pack_share([(3, up_two), (4, down_two)])
    halo_copies += [send_share(0, g, 6, 4, halo_one) for g in range(1, GROUPS)]
    past = []

    def start_past():
        past.append(send(table_past, up_past, at_z(1)))
        past.append(send(table_past, down_past, at_z(-1)))

    halo_copies += forward_far(0, relays, halo_one, {0: start_past})
    kept = pltpu.make_async_copy(
        share.at[pl.ds(0, SHARE)], halo_one.at[pl.ds(0, SHARE)], local_sem.at[1]
    )
    kept.start()
    kept.wait()
    for copy in halo_copies:
        copy.wait_recv()

    def tiles(step, total):
        for i in range(UNROLL):
            e = order[0, step * UNROLL + i]
            product = jnp.dot(
                adjacency[e & 255],
                halo_one[e >> 8],
                preferred_element_type=jnp.float32,
            )
            total = total * keep[0, step * UNROLL + i] + product
            sums[step * UNROLL + i] = total
        return total

    lax.fori_loop(0, TILES // UNROLL, tiles, jnp.zeros((BLOCK, BLOCK), jnp.float32))

    @pl.loop(0, NB)
    def _(b):
        value = own[b] + sums[order[1, b]] * keep[1, b] + bias[...]
        hidden[b] = jnp.maximum(value, 0.0).astype(jnp.bfloat16)

    half = NB // 2
    low, high = pl.ds(0, half), pl.ds(half, half)
    for copy in past:
        copy.wait_recv()
    hop = [
        send(up_past, up_past_two, at_z(1)),
        send(down_past, down_past_two, at_z(-1)),
    ]
    beside = [send(hidden, near_y.at[0], at_y(1)), send(hidden, near_y.at[1], at_y(-1))]

    for copy in halo_copies:
        copy.wait_send()
    pack_share([(0, table_past), (1, up_past), (2, down_past)])
    last_copies = [send_share(1, g, 0, 6, halo_two) for g in range(1, GROUPS)]
    for copies in relays:
        for copy in copies:
            copy.wait_send()
    for copy in hop:
        copy.wait_recv()
    pack_relay(up_past_two, down_past_two)
    relays_two = [send_relay(1, c) for c in range(CHUNKS)]
    for copy in beside:
        copy.wait_recv()
    across = [
        send(near_y.at[0, low], far_y.at[low], at_y(1)),
        send(near_y.at[1, high], far_y.at[high], at_y(-1)),
    ]
    pack_share([(3, up_past_two), (4, down_past_two)])
    last_copies += [send_share(1, g, 6, 4, halo_two) for g in range(1, GROUPS)]
    last_copies += forward_far(1, relays_two, halo_two, {})
    kept = pltpu.make_async_copy(
        share.at[pl.ds(0, SHARE)], halo_two.at[pl.ds(0, SHARE)], local_sem.at[2]
    )
    kept.start()
    for copy in across:
        copy.wait_recv()

    def part(shift):
        return weight[pl.ds(pl.multiple_of(lax.rem(y + shift, NY) * BLOCK, BLOCK), BLOCK), :]

    @pl.loop(0, NB // 4)
    def _(i):
        here = pl.ds(i * 4, 4)
        total = jnp.zeros((4 * BLOCK, BLOCK), jnp.float32)
        for rows, shift in ((hidden, 0), (near_y.at[0], 3), (near_y.at[1], 1), (far_y, 2)):
            total += jnp.dot(
                rows[here].reshape(4 * BLOCK, BLOCK),
                part(shift),
                preferred_element_type=jnp.float32,
            )
        table_two[here] = total.astype(jnp.bfloat16).reshape(4, BLOCK, BLOCK)

    for copy in last_copies:
        copy.wait_recv()
    kept.wait()
    waited = halo_copies + [c for copies in relays for c in copies]
    for copy in started:
        if not any(copy is w for w in waited):
            copy.wait_send()


def exchange(mine, order, keep, bias, weight, table_one, up_one, down_one, table_past, own, adjacency):
    def blocks(*count):
        return pltpu.VMEM((*count, BLOCK, BLOCK), jnp.bfloat16)

    table = jax.ShapeDtypeStruct((NB, BLOCK, BLOCK), jnp.bfloat16)
    return pl.pallas_call(
        exchange_kernel,
        out_shape=(
            table,
            table,
            jax.ShapeDtypeStruct((GROUPS * SHARE, BLOCK, BLOCK), jnp.bfloat16),
        ),
        in_specs=[VMEM, SMEM, SMEM] + [VMEM] * 8,
        out_specs=(VMEM, VMEM, ANY),
        scratch_shapes=[
            pltpu.VMEM((5, GROUPS, 8, 128), jnp.int32),
            pltpu.SMEM((5, GROUPS, 8, 128), jnp.int32),
            *[blocks(NB)] * 6,
            blocks(4, 2 * GROUPS),
            blocks(2, 4, 2 * GROUPS),
            blocks(GROUPS * SHARE),
            blocks(GROUPS * SHARE),
            pltpu.VMEM((TILES, BLOCK, BLOCK), jnp.float32),
            blocks(2, NB),
            blocks(NB),
            pltpu.SemaphoreType.DMA((COPIES,)),
            pltpu.SemaphoreType.DMA((COPIES,)),
            pltpu.SemaphoreType.DMA((3,)),
        ],
        compiler_params=pltpu.CompilerParams(
            vmem_limit_bytes=58 * 2**20, collective_id=0, has_side_effects=True
        ),
        cost_estimate=pl.CostEstimate(
            flops=2 * 256 * BLOCK**3, bytes_accessed=32 << 20, transcendentals=0
        ),
        name="exchange",
    )(mine, order, keep, bias.reshape(1, BLOCK), weight, table_one, up_one, down_one, table_past, own, adjacency)


def along_z(step):
    return [
        (row_of(x, z, k), row_of(x, (z + step) % NZ, k))
        for x in range(NX)
        for z in range(NZ)
        for k in range(2)
    ]


def project(rows, weight):
    return (
        jnp.dot(rows, weight, preferred_element_type=jnp.float32)
        .astype(jnp.bfloat16)
        .reshape(NB, BLOCK, BLOCK)
    )


def local(
    features,
    history,
    weight_one,
    weight_two,
    bias_one,
    bias_two,
    adjacency,
    halo_owner,
    halo_block,
    tile_target,
    tile_source,
    tile_count,
):
    row = lax.axis_index("row")
    ids = jnp.stack([row // 16, (row // 2) % 8, row % 2]).astype(jnp.int32)
    table_one = project(features, weight_one)
    up_one = lax.ppermute(table_one, "row", along_z(1))
    down_one = lax.ppermute(table_one, "row", along_z(-1))
    mine, place = prepare(ids, halo_owner, halo_block)
    lists, counts, order, keep = sort_tiles(tile_target, tile_source, tile_count, place)
    table_past = project(history, weight_two)
    own = gather(0, lists, counts, adjacency, [table_one])
    hidden, table_two, halo_two = exchange(
        mine, order, keep, bias_one, weight_two, table_one, up_one, down_one, table_past, own, adjacency
    )
    embedding = gather(1, lists, counts, adjacency, [table_two, halo_two], bias_two)
    return (
        hidden.reshape(NB * BLOCK, BLOCK),
        embedding.reshape(NB * BLOCK, BLOCK),
    )


def solution(mesh):
    return jax.shard_map(
        local,
        mesh=mesh,
        in_specs=(
            P("row", None),
            P("row", None),
            P(None, "col"),
            P(None, "col"),
            P("col"),
            P("col"),
            P("row", None, None),
            P("row", None),
            P("row", None),
            P("row", None),
            P("row", None),
            P("row"),
        ),
        out_specs=(P("row", "col"), P("row", "col")),
        check_vma=False,
    )
```

time: 379 us -> 212 us (0.56)
  Pallas kernels: 0 us -> 178 us
  blocking collectives: 115 us -> 0 us
  waiting for transfers between devices: 88.4 us -> 1.61 us
  local copies, waits for them, and re-layouts: 72.8 us -> 13.1 us
  matrix products: 56.8 us -> 5.68 us
  between operations: 14.9 us -> 1.44 us
  starting transfers between devices: 18.8 us -> 6.49 us
  other arithmetic: 11.5 us -> 0.6 us
    pallas_call x0 -> x5, Pallas kernels: none -> 178 us  [the longest x1 156 us: exchange(): pl.pallas_call(exchange_kernel, out_shape=(table, table, jax.ShapeDtypeSt...]
    all_to_all x1 -> x0, blocking collectives: 102 us -> none  [local(): lax.all_to_all(proj_past[pick_index], 'row', split_axis=0, concat_axis=0,...]
    all_to_all x2 -> x0, waiting for transfers between devices: 88.3 us -> none  [the longest x1 82.6 us: local(): lax.all_to_all(proj_one[pick_index], 'row', split_axis=0, concat_axis=0,...]
    dot_general x7 -> x2, matrix products: 56.8 us -> 5.68 us  [project(): jnp.dot(rows, weight, preferred_element_type=jnp.float32)]
    gather x6 -> x0, local copies, waits for them, and re-layouts: 34.7 us -> none  [the longest x2 20.4 us: aggregate(): picked = sources[source_ids]]
    dot_general x2 -> x0, local copies, waits for them, and re-layouts: 25.5 us -> none  [aggregate(): jnp.einsum('tab,tbw->taw', adjacency, picked, preferred_element_type=jnp....]
    all_to_all x2 -> x0, starting transfers between devices: 18.8 us -> none  [the longest x1 13 us: local(): lax.all_to_all(wanted, 'row', split_axis=0, concat_axis=0, tiled=True)]
    all_gather x1 -> x0, blocking collectives: 12.6 us -> none  [local(): full_weight = lax.all_gather(weight_two, 'col', axis=1, tiled=True)]
  transfers between devices with their start and end apart: 3 -> 2, of which waited for: 2 -> 1; matrix products, arithmetic and copies ran while one was open for 4% -> 1% of each run, Pallas kernels for 0% -> 8%
where the time goes in v1:
time: 212 us; the launch traced here: 207 us
  Pallas kernels  178 us (84%)
  local copies, waits for them, and re-layouts  13.1 us (6%)
  starting transfers between devices  6.49 us (3%)
  matrix products  5.68 us (3%)
    pallas_call x1, Pallas kernels, exchange(): pl.pallas_call(exchange_kernel, out_shape=(table, table, jax.ShapeDtypeSt...  156 us
    unnamed x35, local copies, waits for them, and re-layouts  13.1 us
    pallas_call x2, Pallas kernels, gather(): pl.pallas_call(functools.partial(gather_kernel, kind, widths, last), out_...  8.92 us
    pallas_call x1, Pallas kernels, sort_tiles(): pl.pallas_call(sort_kernel, out_shape=(jax.ShapeDtypeStruct((2, LIST), jn...  8.56 us
    ppermute x1, starting transfers between devices, local(): down_one = lax.ppermute(table_one, 'row', along_z(-1))  6.49 us
    dot_general x2, matrix products, project(): jnp.dot(rows, weight, preferred_element_type=jnp.float32)  5.68 us
    pallas_call x1, Pallas kernels, prepare(): pl.pallas_call(prepare_kernel, out_shape=(jax.ShapeDtypeStruct((8, 128),...  4.71 us
  transfers between devices with their start and end apart: 2, of which 1 were waited for; matrix products, arithmetic and copies ran while one was open for 1% of the time, Pallas kernels for 8%

profile of v1, /device:TPU:1, one launch (start us, length us, event | category | flops | bytes accessed | tf_op | source)
XLA Modules:
  0.0 207.4 jit_solution(1464823002307154855)
XLA Ops:
  0.6 0.0 copy-start
  0.6 0.9 copy-done
  1.5 3.4 %convolution_convert_fusion.1 = bf16[4096,128]{1,0:T(8,128)(2,1)S(1)} fusion(bf16[4096,512]{1,0:T(8,128)(2,1)} %param.12, bf16[512,128]{1,0:T(8,128)(2,1)S(1)} %copy-done), kind=kOutput, calls=%fused_computation.1 | convolution fusion | flops 537395200 | bytes 5373952 | tf_op jit(solution)/shard_map/dot_general | solution.py:543
  5.0 0.0 copy-start.3
  5.0 6.5 %collective-permute-start.1 = (bf16[32,128,128]{2,1,0:T(8,128)(2,1)S(1)}, bf16[32,128,128]{2,1,0:T(8,128)(2,1)S(1)}, u32[]{:S(2)}, u32[]{:S(2)}) collective-permute-start(bf16[32,128,128]{2,1,0:T(8,128)(2,1)S(1)} %bitcast.13), channel_id=1, source_target_pairs={{0,56},{4,60},{8,0},{12,4},{16,8},{20,12},{24,16},{28,20},{32,24},... | collective-permute-start | bytes 3145736 | tf_op jit(solution)/shard_map/ppermute | solution.py:567
  11.5 0.0 collective-permute-start
  12.1 0.6 pad_add_fusion.ids
  12.7 4.7 %prepare.1 = (s32[8,128]{1,0:T(8,128)}, s32[1,128]{1,0:T(1,128)}) custom-call(s32[3]{0:T(128)} %pad_add_fusion.ids, s32[1,96]{1,0:T(1,128)} %owner.1, s32[1,96]{1,0:T(1,128)} %block.1), custom_call_target="tpu_custom_call" | custom-call | bytes 16777216 | tf_op jit(solution)/shard_map/prepare/pallas_call | solution.py:71
  17.5 8.6 %sort_tiles.1 = (s32[2,200]{1,0:T(2,128)}, s32[1,2]{1,0:T(1,128)}, s32[4,192]{1,0:T(4,128)}, f32[2,192]{1,0:T(2,128)}) custom-call(s32[1,192]{1,0:T(1,128)} %target.1, s32[1,192]{1,0:T(1,128)} %source.1, s32[1]{0:T(128)S(6)} %copy.15.count, s32[1,128]{1,0:T(1,128)} %get-tuple-element.12.place), custom_call_target="tpu_custom_call" | custom-call | bytes 25165824 | tf_op jit(solution)/shard_map/sort_tiles/pallas_call | solution.py:148
  26.0 0.0 copy-start.1
  26.0 2.8 %copy-done.1 = bf16[192,128,128]{2,1,0:T(8,128)(2,1)S(1)} copy-done((bf16[192,128,128]{2,1,0:T(8,128)(2,1)S(1)}, bf16[192,128,128]{2,1,0:T(8,128)(2,1)}, u32[]{:S(2)}) %copy-start.1) | copy-done | bytes 6291480
  28.8 0.6 copy-done.7
  29.4 0.7 copy-done.9
  30.1 2.4 %own_tiles.1.own = f32[32,128,128]{2,1,0:T(8,128)S(1)} custom-call(s32[2,200]{1,0:T(2,128)S(1)} %copy-done.7, s32[1,2]{1,0:T(1,128)S(1)} %copy-done.9, bf16[192,128,128]{2,1,0:T(8,128)(2,1)S(1)} %copy-done.1, bf16[32,128,128]{2,1,0:T(8,128)(2,1)S(1)} %bitcast.15), custom_call_target="tpu_custom_call" | custom-call | flops 268435456 | bytes 16777216 | tf_op jit(solution)/shard_map/own_tiles/pallas_call | solution.py:213
  32.5 0.0 copy-done.3
  32.5 0.0 copy-done.12
  32.5 0.0 copy-done.16
  32.5 0.0 copy-start.4
  32.5 2.2 %convolution_convert_fusion = bf16[4096,128]{1,0:T(8,128)(2,1)} fusion(bf16[4096,512]{1,0:T(8,128)(2,1)S(1)} %copy-done.12, bf16[512,128]{1,0:T(8,128)(2,1)S(1)} %copy-done.16), kind=kOutput, calls=%fused_computation | convolution fusion | flops 537395200 | bytes 5373952 | tf_op jit(solution)/shard_map/dot_general | solution.py:543
  34.8 0.0 collective-permute-done.1.down_one
  34.8 1.6 collective-permute-done.up_one
  36.4 0.0 copy-done.4
  36.4 0.0 copy-done.13
  36.4 1.0 copy-done.14
  37.4 156.3 %exchange.1 = (bf16[32,128,128]{2,1,0:T(8,128)(2,1)}, bf16[32,128,128]{2,1,0:T(8,128)(2,1)}, bf16[128,128,128]{2,1,0:T(8,128)(2,1)}) custom-call(s32[8,128]{1,0:T(8,128)} %get-tuple-element.11.mine, s32[4,192]{1,0:T(4,128)} %get-tuple-element.13.order, f32[2,192]{1,0:T(2,128)} %get-tuple-element.14.keep, f32[1,128]{1,0:T(1,128)} %bitcast.21, ...), custom_call_target="tpu_custom_call" | custom-call | flops 1073741824 | bytes 33554432 | tf_op jit(solution)/shard_map/exchange/pallas_call | solution.py:498
  193.7 0.0 copy-done.8
  193.7 0.0 copy-start.2
  193.7 2.8 %copy-done.2 = bf16[192,128,128]{2,1,0:T(8,128)(2,1)S(1)} copy-done((bf16[192,128,128]{2,1,0:T(8,128)(2,1)S(1)}, bf16[192,128,128]{2,1,0:T(8,128)(2,1)}, u32[]{:S(2)}) %copy-start.2) | copy-done | bytes 6291480
  196.5 2.2 %copy-done.5 = bf16[128,128,128]{2,1,0:T(8,128)(2,1)S(1)} copy-done((bf16[128,128,128]{2,1,0:T(8,128)(2,1)S(1)}, bf16[128,128,128]{2,1,0:T(8,128)(2,1)}, u32[]{:S(2)}) %copy-start.5) | copy-done | bytes 4194328
  198.7 1.2 copy-done.6
  199.9 6.5 %all_tiles.1 = bf16[32,128,128]{2,1,0:T(8,128)(2,1)} custom-call(s32[2,200]{1,0:T(2,128)S(1)} %copy-done.8, s32[1,2]{1,0:T(1,128)S(1)} %copy-done.10, bf16[192,128,128]{2,1,0:T(8,128)(2,1)S(1)} %copy-done.2, bf16[32,128,128]{2,1,0:T(8,128)(2,1)S(1)} %copy-done.6, bf16[128,128,128]{2,1,0:T(8,128)(2,1)S(1)} %copy-done.5, f32[1,128]{1,0:T(1,128)S(1)} %bitcast.17), custom_call_target="tpu_custom_call" | custom-call | flops 268435456 | bytes 16777216 | tf_op jit(solution)/shard_map/all_tiles/pallas_call | solution.py:213
  206.5 1.0 copy.16
  (15 shorter events, 0.0 us)
Async XLA Ops:
  0.6 0.9 copy-start
  5.0 27.5 %copy-start.3 = (bf16[4096,128]{1,0:T(8,128)(2,1)}, bf16[4096,128]{1,0:T(8,128)(2,1)S(1)}, u32[]{:S(2)}) copy-start(bf16[4096,128]{1,0:T(8,128)(2,1)S(1)} %convolution_convert_fusion.1) | copy-start | bytes 3145732
  5.0 29.8 %collective-permute-start.1 = (bf16[32,128,128]{2,1,0:T(8,128)(2,1)S(1)}, bf16[32,128,128]{2,1,0:T(8,128)(2,1)S(1)}, u32[]{:S(2)}, u32[]{:S(2)}) collective-permute-start(bf16[32,128,128]{2,1,0:T(8,128)(2,1)S(1)} %bitcast.13), channel_id=1, source_target_pairs={{0,56},{4,60},{8,0},{12,4},{16,8},{20,12},{24,16},{28,20},{32,24},... | collective-permute-start | bytes 3145736 | tf_op jit(solution)/shard_map/ppermute | solution.py:567
  11.5 24.9 %collective-permute-start = (bf16[32,128,128]{2,1,0:T(8,128)(2,1)S(1)}, bf16[32,128,128]{2,1,0:T(8,128)(2,1)S(1)}, u32[]{:S(2)}, u32[]{:S(2)}) collective-permute-start(bf16[32,128,128]{2,1,0:T(8,128)(2,1)S(1)} %bitcast.14), channel_id=1, source_target_pairs={{0,8},{4,12},{8,16},{12,20},{16,24},{20,28},{24,32},{28,36},{32,40... | collective-permute-start | bytes 3145736 | tf_op jit(solution)/shard_map/ppermute | solution.py:566
  26.0 2.8 %copy-start.1 = (bf16[192,128,128]{2,1,0:T(8,128)(2,1)S(1)}, bf16[192,128,128]{2,1,0:T(8,128)(2,1)}, u32[]{:S(2)}) copy-start(bf16[192,128,128]{2,1,0:T(8,128)(2,1)} %refs_2_.3) | copy-start | bytes 18874372
  28.8 0.6 copy-start.7
  29.4 0.7 copy-start.9
  30.1 2.4 %copy-start.12 = (bf16[4096,512]{1,0:T(8,128)(2,1)S(1)}, bf16[4096,512]{1,0:T(8,128)(2,1)}, u32[]{:S(2)}) copy-start(bf16[4096,512]{1,0:T(8,128)(2,1)} %param.13) | copy-start | bytes 12582916
  30.1 2.4 %copy-start.16 = (bf16[512,128]{1,0:T(8,128)(2,1)S(1)}, bf16[512,128]{1,0:T(8,128)(2,1)}, u32[]{:S(2)}) copy-start(bf16[512,128]{1,0:T(8,128)(2,1)} %weight.1) | copy-start | bytes 393220
  32.5 3.9 %copy-start.4 = (f32[32,128,128]{2,1,0:T(8,128)}, f32[32,128,128]{2,1,0:T(8,128)S(1)}, u32[]{:S(2)}) copy-start(f32[32,128,128]{2,1,0:T(8,128)S(1)} %own_tiles.1.own) | copy-start | bytes 6291460
  34.8 1.6 copy-start.13
  36.4 1.0 copy-start.14
  37.4 156.3 %copy-start.8 = (s32[2,200]{1,0:T(2,128)S(1)}, s32[2,200]{1,0:T(2,128)}, u32[]{:S(2)}) copy-start(s32[2,200]{1,0:T(2,128)} %get-tuple-element.15.refs_0_) | copy-start | bytes 4804
  37.4 156.3 %copy-start.10 = (s32[1,2]{1,0:T(1,128)S(1)}, s32[1,2]{1,0:T(1,128)}, u32[]{:S(2)}) copy-start(s32[1,2]{1,0:T(1,128)} %get-tuple-element.16.refs_1_) | copy-start | bytes 28
  37.4 156.3 %copy-start.11 = (f32[128]{0:T(128)S(1)}, f32[128]{0:T(128)}, u32[]{:S(2)}) copy-start(f32[128]{0:T(128)} %param.17) | copy-start | bytes 1540
  193.7 2.8 %copy-start.2 = (bf16[192,128,128]{2,1,0:T(8,128)(2,1)S(1)}, bf16[192,128,128]{2,1,0:T(8,128)(2,1)}, u32[]{:S(2)}) copy-start(bf16[192,128,128]{2,1,0:T(8,128)(2,1)} %refs_2_.3) | copy-start | bytes 18874372
  196.5 2.2 %copy-start.5 = (bf16[128,128,128]{2,1,0:T(8,128)(2,1)S(1)}, bf16[128,128,128]{2,1,0:T(8,128)(2,1)}, u32[]{:S(2)}) copy-start(bf16[128,128,128]{2,1,0:T(8,128)(2,1)} %get-tuple-element.19.refs_4_) | copy-start | bytes 12582916
  198.7 1.2 copy-start.6
  199.9 6.6 %copy-start.15 = (bf16[32,128,128]{2,1,0:T(8,128)(2,1)S(1)}, bf16[32,128,128]{2,1,0:T(8,128)(2,1)}, u32[]{:S(2)}) copy-start(bf16[32,128,128]{2,1,0:T(8,128)(2,1)} %get-tuple-element.17) | copy-start | bytes 3145732

commit v2 on v1

v2 whole, which is shorter than its diff:
```python
import jax
import jax.numpy as jnp
from jax import lax
from jax.experimental import pallas as pl
from jax.experimental.pallas import tpu as pltpu
from jax.sharding import PartitionSpec as P

BLOCK = 128
NB = 32
TILES = 192
HALO = 96
NX, NZ, NY = 4, 8, 4
GROUPS = 8
SHARE = 16
UNROLL = 8
FIRSTS = (4, 2, 6, 0)
MESH = pl.DeviceIdType.MESH

STEPS = (0, 7, 1, 6, 2, 5, 3, 4)

SMEM = pl.BlockSpec(memory_space=pltpu.SMEM)
VMEM = pl.BlockSpec(memory_space=pltpu.VMEM)
ANY = pl.BlockSpec(memory_space=pl.ANY)


def row_of(x, z, k):
    return x * (NZ * 2) + z * 2 + k


def member(x, k, group):
    dx, dk = group // 2, group % 2
    return lax.rem(x + dx, NX), k + dk - 2 * k * dk


def prepare_kernel(ids, owner, block, wanted, place):
    x, z, k = ids[0], ids[1], ids[2]

    @pl.loop(0, 128, unroll=8)
    def _(i):
        wanted[0, i] = 0
        place[0, i] = 0

    @pl.loop(0, 64, unroll=8)
    def _(i):
        wanted[1, i] = 0

    @pl.loop(0, HALO)
    def _(h):
        named = owner[0, h]
        o = jnp.maximum(named, 0)
        live = named >= 0
        nth = jnp.where(live, wanted[1, o], 0)
        wanted[1, o] = jnp.where(live, nth + 1, wanted[1, o])
        at = 2 * o + nth
        wanted[0, at] = jnp.where(live, block[0, h], wanted[0, at])
        ox, oz, ok = o // 16, (o // 2) % 8, o % 2
        group = lax.rem(x - ox + NX, NX) * 2 + (k + ok - 2 * k * ok)
        step = lax.rem(oz - z + NZ, NZ)
        spot = jnp.int32(0)
        for i, s in enumerate(STEPS):
            spot = jnp.where(step == s, 2 * i, spot)
        place[0, h] = group * SHARE + spot + nth


def prepare(ids, owner, block):
    return pl.pallas_call(
        prepare_kernel,
        out_shape=(
            jax.ShapeDtypeStruct((8, 128), jnp.int32),
            jax.ShapeDtypeStruct((1, 128), jnp.int32),
        ),
        in_specs=[SMEM] * 3,
        out_specs=(SMEM, SMEM),
        cost_estimate=pl.CostEstimate(flops=0, bytes_accessed=16 << 20, transcendentals=0),
        name="prepare",
    )(ids, owner, block)


def sort_kernel(target, source, count, place, order, keep):
    live = count[0]

    @pl.loop(0, TILES, unroll=8)
    def _(i):
        keep[0, i] = 1.0

    @pl.loop(0, NB + 1, unroll=11)
    def _(b):
        order[2, b] = 0

    @pl.loop(0, TILES, unroll=8)
    def _(t):
        b = jnp.where(t < live, target[0, t], NB)
        order[2, b] = order[2, b] + 1

    def start(b, at):
        many = order[2, b]
        order[2, b] = at
        order[1, b] = jnp.maximum(at + many - 1, 0)
        keep[1, b] = jnp.where(many > 0, 1.0, 0.0)
        first = jnp.minimum(at, TILES - 1)
        keep[0, first] = jnp.where(many > 0, 0.0, keep[0, first])
        return at + many

    lax.fori_loop(0, NB + 1, start, jnp.int32(0))

    @pl.loop(0, TILES, unroll=8)
    def _(t):
        b = jnp.where(t < live, target[0, t], NB)
        s = source[0, t]
        halo = NB + place[0, jnp.clip(s - NB, 0, HALO - 1)]
        at = order[2, b]
        order[0, at] = t | (jnp.where(s < NB, s, halo) << 8)
        order[2, b] = at + 1


def sort_tiles(target, source, count, place):
    return pl.pallas_call(
        sort_kernel,
        out_shape=(
            jax.ShapeDtypeStruct((3, TILES), jnp.int32),
            jax.ShapeDtypeStruct((2, TILES), jnp.float32),
        ),
        in_specs=[SMEM] * 4,
        out_specs=(SMEM,) * 2,
        cost_estimate=pl.CostEstimate(flops=0, bytes_accessed=24 << 20, transcendentals=0),
        name="sort_tiles",
    )(target, source, count, place)


COPIES = 128


def exchange_kernel(
    mine,
    order,
    keep,
    bias_one,
    bias_two,
    weight,
    table_one,
    up_one,
    down_one,
    table_past,
    adjacency_at,
    hidden,
    embedding,
    wanted_all,
    wanted,
    up_two,
    down_two,
    up_past,
    down_past,
    up_past_two,
    down_past_two,
    relay_out,
    relay_in,
    share,
    sources_one,
    sources_two,
    adjacency,
    sums,
    near_y,
    far_y,
    send_sem,
    recv_sem,
    local_sem,
):
    row = lax.axis_index("row")
    y = lax.axis_index("col")
    x, z, k = row // 16, lax.rem(row // 2, NZ), lax.rem(row, 2)
    me = x * 2 + k
    used = [0]

    def at_z(step):
        return (row_of(x, lax.rem(z + step + NZ, NZ), k), y)

    def at_slab(group):
        ox, ok = member(x, k, group)
        return (row_of(ox, z, ok), y)

    def at_y(step):
        return (row, lax.rem(y + step + NY, NY))

    peers = [at_z(s) for s in (1, -1, 2, -2)]
    peers += [at_slab(g) for g in range(1, GROUPS)]
    peers += [at_y(s) for s in (1, -1)]

    barrier = pltpu.get_barrier_semaphore()
    for peer in peers:
        pl.semaphore_signal(barrier, inc=1, device_id=peer, device_id_type=MESH)
    pl.semaphore_wait(barrier, len(peers))

    started = []

    def send(src, dst, device):
        i = used[0]
        used[0] += 1
        copy = pltpu.make_async_remote_copy(
            src_ref=src,
            dst_ref=dst,
            send_sem=send_sem.at[i],
            recv_sem=recv_sem.at[i],
            device_id=device,
            device_id_type=MESH,
        )
        copy.start()
        started.append(copy)
        return copy

    def arrived(copies):
        for copy in copies:
            copy.wait_recv()

    def piece(i, count):
        return pl.ds(i * (NB // count), NB // count)

    asks = [send(mine, wanted_all.at[2, me], at_slab(g)) for g in range(1, GROUPS)]
    hop = [
        [send(up_one.at[p], up_two.at[p], at_z(1)), send(down_one.at[p], down_two.at[p], at_z(-1))]
        for p in (piece(0, 2), piece(1, 2))
    ]
    to_near = pltpu.make_async_copy(adjacency_at, adjacency, local_sem.at[0])
    to_near.start()
    to_sources = pltpu.make_async_copy(table_one, sources_one.at[pl.ds(0, NB)], local_sem.at[1])
    to_sources.start()
    wanted_all[2, me] = mine[...]
    arrived(asks)
    asks = [send(wanted_all.at[2], wanted_all.at[2 - s], at_z(s)) for s in (1, -1, 2, -2)]
    arrived(asks)
    to_scalars = pltpu.make_async_copy(wanted_all, wanted, local_sem.at[2])
    to_scalars.start()
    to_scalars.wait()

    def pick(shift, group, step, slot):
        ox, ok = member(x, k, group)
        o = row_of(x, lax.rem(z + step + NZ, NZ), k)
        return wanted[2 + shift, ox * 2 + ok, 0, 2 * o + slot]

    def pack_share(parts):
        @pl.loop(0, GROUPS)
        def _(g):
            for i, table in parts:
                for slot in range(2):
                    share[g * SHARE + 2 * i + slot] = table[pick(0, g, STEPS[i], slot)]

    def send_share(g, start, size, sources):
        at = g * SHARE + start
        return send(share.at[pl.ds(at, size)], sources.at[pl.ds(NB + at, size)], at_slab(g))

    def pack_relay(up, down):
        @pl.loop(0, GROUPS)
        def _(g):
            for side, (table, sign) in enumerate(((up, 1), (down, -1))):
                for slot in range(2):
                    relay_out[side, g * 2 + slot] = table[pick(sign, g, -2 * sign, slot)]
                relay_out[2 + side, g] = table[pick(2 * sign, g, -2 * sign, side)]

    def send_relay(layer, first):
        near, far = pl.ds(first * 2, 4), pl.ds(first, 2)
        copies = []
        for side, sign in ((0, 1), (1, -1)):
            copies.append(send(relay_out.at[2 + side, far], relay_in.at[layer, 2 + side, far], at_z(2 * sign)))
            copies.append(send(relay_out.at[side, near], relay_in.at[layer, side, near], at_z(sign)))
        return copies

    def pack_far(layer, g):
        at = g * SHARE
        share[at + 10] = relay_in[layer, 0, 2 * g]
        share[at + 11] = relay_in[layer, 0, 2 * g + 1]
        share[at + 12] = relay_in[layer, 1, 2 * g]
        share[at + 13] = relay_in[layer, 1, 2 * g + 1]
        share[at + 14] = relay_in[layer, 2, g]
        share[at + 15] = relay_in[layer, 3, g]

    def forward_far(layer, relays, sources, between):
        copies = []
        for first, then in zip(FIRSTS, between):
            arrived(relays[first])
            for g in (first, first + 1):
                pack_far(layer, g)
                if g > 0:
                    copies.append(send_share(g, 10, 6, sources))
            then()
        return copies

    def keep_own(sources, i):
        copy = pltpu.make_async_copy(
            share.at[pl.ds(0, SHARE)], sources.at[pl.ds(NB, SHARE)], local_sem.at[i]
        )
        copy.start()
        copy.wait()

    def multiply(sources):
        def some(step, total):
            for i in range(UNROLL):
                e = order[0, step * UNROLL + i]
                product = jnp.dot(
                    adjacency[e & 255],
                    sources[e >> 8],
                    preferred_element_type=jnp.float32,
                )
                total = total * keep[0, step * UNROLL + i] + product
                sums[step * UNROLL + i] = total
            return total

        lax.fori_loop(0, TILES // UNROLL, some, jnp.zeros((BLOCK, BLOCK), jnp.float32))

    def summed(b):
        return sums[order[1, b]] * keep[1, b]

    others = range(1, GROUPS)

    pack_share([(0, table_one), (1, up_one), (2, down_one)])
    halo_copies = [send_share(g, 0, 6, sources_one) for g in others]
    past = []

    def start_past():
        p = piece(len(past), 4)
        past.append(
            [send(table_past.at[p], up_past.at[p], at_z(1)), send(table_past.at[p], down_past.at[p], at_z(-1))]
        )

    arrived(hop[0])
    start_past()
    arrived(hop[1])
    pack_relay(up_two, down_two)
    relays = {first: send_relay(0, first) for first in FIRSTS}
    pack_share([(3, up_two), (4, down_two)])
    halo_copies += [send_share(g, 6, 4, sources_one) for g in others]

    def start_two():
        start_past()
        start_past()

    halo_copies += forward_far(
        0, relays, sources_one, (lambda: None, start_past, start_two, lambda: None)
    )
    hop = []
    for i in range(4):
        p = piece(i, 4)
        arrived(past[i])
        hop.append(
            [send(up_past.at[p], up_past_two.at[p], at_z(1)), send(down_past.at[p], down_past_two.at[p], at_z(-1))]
        )
    keep_own(sources_one, 3)
    arrived(halo_copies)
    to_near.wait()
    to_sources.wait()
    multiply(sources_one)

    @pl.loop(0, NB)
    def _(b):
        hidden[b] = jnp.maximum(summed(b) + bias_one[...], 0.0).astype(jnp.bfloat16)

    low, high = piece(0, 2), piece(1, 2)
    from_below = [send(hidden.at[low], near_y.at[0, low], at_y(1))]
    from_above = [send(hidden.at[high], near_y.at[1, high], at_y(-1))]
    from_below.append(send(hidden.at[high], near_y.at[0, high], at_y(1)))
    from_above.append(send(hidden.at[low], near_y.at[1, low], at_y(-1)))

    for copy in halo_copies:
        copy.wait_send()
    pack_share([(0, table_past), (1, up_past), (2, down_past)])
    last_copies = [send_share(g, 0, 6, sources_two) for g in others]
    for copies in relays.values():
        for copy in copies:
            copy.wait_send()
    arrived([from_below[0], from_above[0]])
    across = [
        send(near_y.at[0, low], far_y.at[low], at_y(1)),
        send(near_y.at[1, high], far_y.at[high], at_y(-1)),
    ]
    for copies in hop:
        arrived(copies)
    pack_relay(up_past_two, down_past_two)
    relays_two = {first: send_relay(1, first) for first in FIRSTS}
    pack_share([(3, up_past_two), (4, down_past_two)])
    last_copies += [send_share(g, 6, 4, sources_two) for g in others]
    arrived([from_below[1], from_above[1], *across])

    def part(shift):
        return weight[pl.ds(pl.multiple_of(lax.rem(y + shift, NY) * BLOCK, BLOCK), BLOCK), :]

    @pl.loop(0, NB // 4)
    def _(i):
        here = pl.ds(i * 4, 4)
        total = jnp.zeros((4 * BLOCK, BLOCK), jnp.float32)
        for rows, shift in ((hidden, 0), (near_y.at[0], 3), (near_y.at[1], 1), (far_y, 2)):
            total += jnp.dot(
                rows[here].reshape(4 * BLOCK, BLOCK),
                part(shift),
                preferred_element_type=jnp.float32,
            )
        sources_two[here] = total.astype(jnp.bfloat16).reshape(4, BLOCK, BLOCK)

    last_copies += forward_far(1, relays_two, sources_two, (lambda: None,) * 4)
    keep_own(sources_two, 4)
    arrived(last_copies)
    multiply(sources_two)

    @pl.loop(0, NB)
    def _(b):
        embedding[b] = (summed(b) + bias_two[...]).astype(jnp.bfloat16)

    waited = halo_copies + [c for copies in relays.values() for c in copies]
    for copy in started:
        if not any(copy is w for w in waited):
            copy.wait_send()


def exchange(mine, order, keep, bias_one, bias_two, weight, table_one, up_one, down_one, table_past, adjacency):
    def blocks(*count):
        return pltpu.VMEM((*count, BLOCK, BLOCK), jnp.bfloat16)

    table = jax.ShapeDtypeStruct((NB, BLOCK, BLOCK), jnp.bfloat16)
    return pl.pallas_call(
        exchange_kernel,
        out_shape=(table, table),
        in_specs=[VMEM, SMEM, SMEM] + [VMEM] * 7 + [ANY],
        out_specs=(VMEM, VMEM),
        scratch_shapes=[
            pltpu.VMEM((5, GROUPS, 8, 128), jnp.int32),
            pltpu.SMEM((5, GROUPS, 8, 128), jnp.int32),
            *[blocks(NB)] * 6,
            blocks(4, 2 * GROUPS),
            blocks(2, 4, 2 * GROUPS),
            blocks(GROUPS * SHARE),
            blocks(NB + GROUPS * SHARE),
            blocks(NB + GROUPS * SHARE),
            blocks(TILES),
            pltpu.VMEM((TILES, BLOCK, BLOCK), jnp.float32),
            blocks(2, NB),
            blocks(NB),
            pltpu.SemaphoreType.DMA((COPIES,)),
            pltpu.SemaphoreType.DMA((COPIES,)),
            pltpu.SemaphoreType.DMA((5,)),
        ],
        compiler_params=pltpu.CompilerParams(
            vmem_limit_bytes=60 * 2**20, collective_id=0, has_side_effects=True
        ),
        cost_estimate=pl.CostEstimate(
            flops=2 * 512 * BLOCK**3, bytes_accessed=32 << 20, transcendentals=0
        ),
        name="exchange",
    )(
        mine,
        order,
        keep,
        bias_one.reshape(1, BLOCK),
        bias_two.reshape(1, BLOCK),
        weight,
        table_one,
        up_one,
        down_one,
        table_past,
        adjacency,
    )


def along_z(step):
    return [
        (row_of(x, z, k), row_of(x, (z + step) % NZ, k))
        for x in range(NX)
        for z in range(NZ)
        for k in range(2)
    ]


def project(rows, weight):
    return (
        jnp.dot(rows, weight, preferred_element_type=jnp.float32)
        .astype(jnp.bfloat16)
        .reshape(NB, BLOCK, BLOCK)
    )


def local(
    features,
    history,
    weight_one,
    weight_two,
    bias_one,
    bias_two,
    adjacency,
    halo_owner,
    halo_block,
    tile_target,
    tile_source,
    tile_count,
):
    row = lax.axis_index("row")
    ids = jnp.stack([row // 16, (row // 2) % 8, row % 2]).astype(jnp.int32)
    table_one = project(features, weight_one)
    up_one = lax.ppermute(table_one, "row", along_z(1))
    down_one = lax.ppermute(table_one, "row", along_z(-1))
    mine, place = prepare(ids, halo_owner, halo_block)
    order, keep = sort_tiles(tile_target, tile_source, tile_count, place)
    table_past = project(history, weight_two)
    hidden, embedding = exchange(
        mine, order, keep, bias_one, bias_two, weight_two, table_one, up_one, down_one, table_past, adjacency
    )
    return (
        hidden.reshape(NB * BLOCK, BLOCK),
        embedding.reshape(NB * BLOCK, BLOCK),
    )


def solution(mesh):
    return jax.shard_map(
        local,
        mesh=mesh,
        in_specs=(
            P("row", None),
            P("row", None),
            P(None, "col"),
            P(None, "col"),
            P("col"),
            P("col"),
            P("row", None, None),
            P("row", None),
            P("row", None),
            P("row", None),
            P("row", None),
            P("row"),
        ),
        out_specs=(P("row", "col"), P("row", "col")),
        check_vma=False,
    )
```

time: 212 us -> 197 us (0.929); the launches traced: 207 us -> 195 us
  Pallas kernels: 178 us -> 163 us
  waiting for transfers between devices: 1.61 us -> 9.37 us
  local copies, waits for them, and re-layouts: 13.1 us -> 6.39 us
  matrix products: 5.68 us -> 7.9 us
    pallas_call x4 -> x2, Pallas kernels: 174 us -> 159 us  [the longest x1 154 us: exchange(): pl.pallas_call(exchange_kernel, out_shape=(table, table), in_specs=[VMEM,...]
    unnamed x35 -> x12, local copies, waits for them, and re-layouts: 13.1 us -> 6.39 us
    ppermute x1, waiting for transfers between devices: 0.01 us -> 6.28 us  [local(): down_one = lax.ppermute(table_one, 'row', along_z(-1))]
    dot_general x2, matrix products: 5.68 us -> 7.9 us  [project(): jnp.dot(rows, weight, preferred_element_type=jnp.float32)]
  transfers between devices with their start and end apart: 2 -> 2, of which waited for: 1 -> 2; matrix products, arithmetic and copies ran while one was open for 1% -> 3% of each run, Pallas kernels for 8% -> 5%
where the time goes in v2:
time: 197 us; the launch traced here: 195 us
  Pallas kernels  163 us (83%)
  waiting for transfers between devices  9.37 us (5%)
  matrix products  7.9 us (4%)
  starting transfers between devices  6.49 us (3%)
  local copies, waits for them, and re-layouts  6.39 us (3%)
    pallas_call x1, Pallas kernels, exchange(): pl.pallas_call(exchange_kernel, out_shape=(table, table), in_specs=[VMEM,...  154 us
    dot_general x2, matrix products, project(): jnp.dot(rows, weight, preferred_element_type=jnp.float32)  7.9 us
    ppermute x1, starting transfers between devices, local(): down_one = lax.ppermute(table_one, 'row', along_z(-1))  6.49 us
    unnamed x12, local copies, waits for them, and re-layouts  6.39 us
    ppermute x1, waiting for transfers between devices, local(): down_one = lax.ppermute(table_one, 'row', along_z(-1))  6.28 us
    pallas_call x1, Pallas kernels, sort_tiles(): pl.pallas_call(sort_kernel, out_shape=(jax.ShapeDtypeStruct((3, TILES), j...  5.05 us
    pallas_call x1, Pallas kernels, prepare(): pl.pallas_call(prepare_kernel, out_shape=(jax.ShapeDtypeStruct((8, 128),...  4.71 us
  transfers between devices with their start and end apart: 2, of which 2 were waited for; matrix products, arithmetic and copies ran while one was open for 3% of the time, Pallas kernels for 5%

profile of v2, /device:TPU:1, one launch (start us, length us, event | category | flops | bytes accessed | tf_op | source)
XLA Modules:
  0.0 195.5 jit_solution(10034495087284460877)
XLA Ops:
  0.6 0.0 copy-start
  0.6 0.0 copy-start.4
  0.7 0.9 copy-done
  1.5 3.4 %convolution_convert_fusion.1 = bf16[4096,128]{1,0:T(8,128)(2,1)S(1)} fusion(bf16[4096,512]{1,0:T(8,128)(2,1)} %param.12, bf16[512,128]{1,0:T(8,128)(2,1)S(1)} %copy-done), kind=kOutput, calls=%fused_computation.1 | convolution fusion | flops 537395200 | bytes 5373952 | tf_op jit(solution)/shard_map/dot_general | solution.py:471
  5.0 0.0 copy-start.1
  5.0 6.5 %collective-permute-start.1 = (bf16[32,128,128]{2,1,0:T(8,128)(2,1)S(1)}, bf16[32,128,128]{2,1,0:T(8,128)(2,1)S(1)}, u32[]{:S(2)}, u32[]{:S(2)}) collective-permute-start(bf16[32,128,128]{2,1,0:T(8,128)(2,1)S(1)} %bitcast.13), channel_id=1, source_target_pairs={{0,56},{4,60},{8,0},{12,4},{16,8},{20,12},{24,16},{28,20},{32,24},... | collective-permute-start | bytes 3145736 | tf_op jit(solution)/shard_map/ppermute | solution.py:495
  11.5 0.0 collective-permute-start
  12.1 0.6 pad_add_fusion.ids
  12.8 4.7 %prepare.1 = (s32[8,128]{1,0:T(8,128)}, s32[1,128]{1,0:T(1,128)}) custom-call(s32[3]{0:T(128)} %pad_add_fusion.ids, s32[1,96]{1,0:T(1,128)} %owner.1, s32[1,96]{1,0:T(1,128)} %block.1), custom_call_target="tpu_custom_call" | custom-call | bytes 16777216 | tf_op jit(solution)/shard_map/prepare/pallas_call | solution.py:66
  17.5 5.1 %sort_tiles.1 = (s32[3,192]{1,0:T(4,128)}, f32[2,192]{1,0:T(2,128)}) custom-call(s32[1,192]{1,0:T(1,128)} %target.1, s32[1,192]{1,0:T(1,128)} %source.1, s32[1]{0:T(128)S(6)} %copy.16.count, s32[1,128]{1,0:T(1,128)} %get-tuple-element.9.place), custom_call_target="tpu_custom_call" | custom-call | bytes 25165824 | tf_op jit(solution)/shard_map/sort_tiles/pallas_call | solution.py:117
  22.6 0.0 copy-done.4
  22.6 4.5 %convolution_convert_fusion = bf16[4096,128]{1,0:T(8,128)(2,1)} fusion(bf16[4096,512]{1,0:T(8,128)(2,1)} %param.13, bf16[512,128]{1,0:T(8,128)(2,1)S(1)} %copy-done.4), kind=kOutput, calls=%fused_computation | convolution fusion | flops 537395200 | bytes 5373952 | tf_op jit(solution)/shard_map/dot_general | solution.py:471
  27.0 6.3 %collective-permute-done.1.down_one = bf16[32,128,128]{2,1,0:T(8,128)(2,1)S(1)} collective-permute-done((bf16[32,128,128]{2,1,0:T(8,128)(2,1)S(1)}, bf16[32,128,128]{2,1,0:T(8,128)(2,1)S(1)}, u32[]{:S(2)}, u32[]{:S(2)}) %collective-permute-start.1) | collective-permute-done | bytes 1048608 | tf_op jit(solution)/shard_map/ppermute | solution.py:495
  33.3 0.0 copy-start.2
  33.3 3.1 %collective-permute-done.up_one = bf16[32,128,128]{2,1,0:T(8,128)(2,1)S(1)} collective-permute-done((bf16[32,128,128]{2,1,0:T(8,128)(2,1)S(1)}, bf16[32,128,128]{2,1,0:T(8,128)(2,1)S(1)}, u32[]{:S(2)}, u32[]{:S(2)}) %collective-permute-start) | collective-permute-done | bytes 1048608 | tf_op jit(solution)/shard_map/ppermute | solution.py:494
  36.4 0.0 copy-start.3
  36.4 0.0 copy-done.1
  36.4 0.0 copy-done.2
  36.4 1.0 copy-done.3
  37.4 153.6 %exchange.1 = (bf16[32,128,128]{2,1,0:T(8,128)(2,1)}, bf16[32,128,128]{2,1,0:T(8,128)(2,1)}) custom-call(s32[8,128]{1,0:T(8,128)} %get-tuple-element.8.mine, s32[3,192]{1,0:T(4,128)} %get-tuple-element.10.order, f32[2,192]{1,0:T(2,128)} %get-tuple-element.11.keep, f32[1,128]{1,0:T(1,128)} %bitcast.19, f32[1,128]{1,0:T(1,128)} %bitcast.20, ...), custom_call_target="tpu_custom_call" | custom-call | flops 2147483648 | bytes 33554432 | tf_op jit(solution)/shard_map/exchange/pallas_call | solution.py:416
  191.0 2.3 %copy.17 = bf16[4096,128]{1,0:T(8,128)(2,1)} copy(bf16[4096,128]{1,0:T(8,128)(2,1)} %bitcast.18) | data formatting | bytes 2097152
  193.2 2.3 %copy.18 = bf16[4096,128]{1,0:T(8,128)(2,1)} copy(bf16[4096,128]{1,0:T(8,128)(2,1)} %bitcast.17) | data formatting | bytes 2097152
Async XLA Ops:
  0.6 0.9 copy-start
  0.6 21.9 %copy-start.4 = (bf16[512,128]{1,0:T(8,128)(2,1)S(1)}, bf16[512,128]{1,0:T(8,128)(2,1)}, u32[]{:S(2)}) copy-start(bf16[512,128]{1,0:T(8,128)(2,1)} %weight.1) | copy-start | bytes 393220
  5.0 31.4 %copy-start.1 = (bf16[4096,128]{1,0:T(8,128)(2,1)}, bf16[4096,128]{1,0:T(8,128)(2,1)S(1)}, u32[]{:S(2)}) copy-start(bf16[4096,128]{1,0:T(8,128)(2,1)S(1)} %convolution_convert_fusion.1) | copy-start | bytes 3145732
  5.0 28.3 %collective-permute-start.1 = (bf16[32,128,128]{2,1,0:T(8,128)(2,1)S(1)}, bf16[32,128,128]{2,1,0:T(8,128)(2,1)S(1)}, u32[]{:S(2)}, u32[]{:S(2)}) collective-permute-start(bf16[32,128,128]{2,1,0:T(8,128)(2,1)S(1)} %bitcast.13), channel_id=1, source_target_pairs={{0,56},{4,60},{8,0},{12,4},{16,8},{20,12},{24,16},{28,20},{32,24},... | collective-permute-start | bytes 3145736 | tf_op jit(solution)/shard_map/ppermute | solution.py:495
  11.5 24.9 %collective-permute-start = (bf16[32,128,128]{2,1,0:T(8,128)(2,1)S(1)}, bf16[32,128,128]{2,1,0:T(8,128)(2,1)S(1)}, u32[]{:S(2)}, u32[]{:S(2)}) collective-permute-start(bf16[32,128,128]{2,1,0:T(8,128)(2,1)S(1)} %bitcast.14), channel_id=1, source_target_pairs={{0,8},{4,12},{8,16},{12,20},{16,24},{20,28},{24,32},{28,36},{32,40... | collective-permute-start | bytes 3145736 | tf_op jit(solution)/shard_map/ppermute | solution.py:494
  33.3 3.1 %copy-start.2 = (bf16[32,128,128]{2,1,0:T(8,128)(2,1)}, bf16[32,128,128]{2,1,0:T(8,128)(2,1)S(1)}, u32[]{:S(2)}) copy-start(bf16[32,128,128]{2,1,0:T(8,128)(2,1)S(1)} %collective-permute-done.1.down_one) | copy-start | bytes 3145732
  36.4 1.0 copy-start.3

commit v3 on v2

v3 whole, which is shorter than its diff:
```python
import jax
import jax.numpy as jnp
from jax import lax
from jax.experimental import pallas as pl
from jax.experimental.pallas import tpu as pltpu
from jax.sharding import PartitionSpec as P

BLOCK = 128
NB = 32
TILES = 192
HALO = 96
NX, NZ, NY = 4, 8, 4
GROUPS = 8
SHARE = 16
UNROLL = 8
FIRSTS = (4, 2, 6, 0)
MESH = pl.DeviceIdType.MESH

STEPS = (0, 7, 1, 6, 2, 5, 3, 4)

SMEM = pl.BlockSpec(memory_space=pltpu.SMEM)
VMEM = pl.BlockSpec(memory_space=pltpu.VMEM)
ANY = pl.BlockSpec(memory_space=pl.ANY)


def row_of(x, z, k):
    return x * (NZ * 2) + z * 2 + k


def member(x, k, group):
    dx, dk = group // 2, group % 2
    return lax.rem(x + dx, NX), k + dk - 2 * k * dk


def lane(shape, axis):
    return lax.broadcasted_iota(jnp.int32, shape, axis)


def upright(row):
    n = row.shape[1]
    shape = (n, n)
    diagonal = lane(shape, 0) == lane(shape, 1)
    return jnp.sum(jnp.where(diagonal, row, 0), axis=1, keepdims=True)


def request(x, z, k, owner, block, mine):
    row = owner[...]
    named = upright(row)
    square = (HALO, HALO)
    earlier = lane(square, 1) < lane(square, 0)
    nth = jnp.sum(jnp.where((row == named) & earlier, 1, 0), axis=1, keepdims=True)
    code = jnp.where(named >= 0, 2 * named + nth, -1)
    slots = lane((HALO, 128), 1)
    wanted = jnp.sum(jnp.where(code == slots, upright(block[...]), 0), axis=0, keepdims=True)
    mine[...] = jnp.broadcast_to(wanted, (8, 128))
    o = jnp.maximum(named, 0)
    ox, oz, ok = o >> 4, (o >> 1) & 7, o & 1
    group = ((x - ox) & 3) * 2 + (k + ok - 2 * k * ok)
    step = (oz - z) & 7
    spot = jnp.zeros_like(o)
    for i, s in enumerate(STEPS):
        spot = jnp.where(step == s, 2 * i, spot)
    return group * SHARE + spot + jnp.minimum(nth, 1)


def sort(live, target, source, place, listed, kept):
    line, square = (1, TILES), (TILES, TILES)
    ids = lane(line, 1)
    s = source[...]
    slots = lane((HALO, TILES), 0)
    halo = jnp.sum(jnp.where(slots == s - NB, place, 0), axis=0, keepdims=True)
    at = jnp.where(s < NB, s, halo + NB)
    entry = upright(ids + 256 * at)
    row = jnp.where(ids < live, target[...], NB)
    goal = upright(row)
    key = row * 256 + ids
    rank = jnp.sum(jnp.where(key < upright(key), 1, 0), axis=1, keepdims=True)
    here = rank == lane(square, 1)
    order = jnp.sum(jnp.where(here, entry, 0), axis=0, keepdims=True)
    goals = jnp.sum(jnp.where(here, goal, 0), axis=0, keepdims=True)
    before = jnp.sum(jnp.where(goal < goals, 1, 0), axis=0, keepdims=True)
    listed[0:1, 0:TILES] = order
    kept[0:1, 0:TILES] = jnp.where(before == ids, 0.0, 1.0)
    blocks = lane((TILES, 128), 1)
    upto = jnp.sum(jnp.where(goal <= blocks, 1, 0), axis=0, keepdims=True)
    many = jnp.sum(jnp.where(goal == blocks, 1, 0), axis=0, keepdims=True)
    listed[1:2, 0:128] = jnp.maximum(upto - 1, 0)
    kept[1:2, 0:128] = jnp.where(many > 0, 1.0, 0.0)


COPIES = 128


def exchange_kernel(
    count,
    owner,
    block,
    target,
    source,
    bias_one,
    bias_two,
    first_weight,
    weight,
    features,
    history,
    adjacency_at,
    hidden,
    embedding,
    mine,
    listed,
    kept,
    order,
    keep,
    wanted_all,
    wanted,
    stage,
    table_one,
    table_past,
    up_one,
    down_one,
    up_two,
    down_two,
    up_past,
    down_past,
    up_past_two,
    down_past_two,
    relay_out,
    relay_in,
    share,
    sources_one,
    sources_two,
    adjacency,
    sums,
    near_y,
    far_y,
    send_sem,
    recv_sem,
    local_sem,
):
    row = lax.axis_index("row")
    y = lax.axis_index("col")
    x, z, k = row // 16, lax.rem(row // 2, NZ), lax.rem(row, 2)
    me = x * 2 + k
    used = [0]

    def at_z(step):
        return (row_of(x, lax.rem(z + step + NZ, NZ), k), y)

    def at_slab(group):
        ox, ok = member(x, k, group)
        return (row_of(ox, z, ok), y)

    def at_y(step):
        return (row, lax.rem(y + step + NY, NY))

    peers = [at_z(s) for s in (1, -1, 2, -2)]
    peers += [at_slab(g) for g in range(1, GROUPS)]
    peers += [at_y(s) for s in (1, -1)]

    barrier = pltpu.get_barrier_semaphore()
    for peer in peers:
        pl.semaphore_signal(barrier, inc=1, device_id=peer, device_id_type=MESH)

    rows = NB * BLOCK // 4
    pieces = [(table, w, at, i) for table, w, at in ((table_one, first_weight, features), (table_past, weight, history)) for i in range(4)]
    fetches = [
        pltpu.make_async_copy(at.at[pl.ds(i * rows, rows)], stage.at[n % 2], local_sem.at[5 + n])
        for n, (_, _, at, i) in enumerate(pieces)
    ]

    def project(n):
        table, w, _, i = pieces[n]
        fetches[n].wait()

        @pl.loop(0, NB // 8)
        def _(j):
            part = stage[n % 2, pl.ds(j * 2 * BLOCK, 2 * BLOCK)]
            product = jnp.dot(part, w[...], preferred_element_type=jnp.float32)
            table[pl.ds(i * (NB // 4) + 2 * j, 2)] = product.astype(jnp.bfloat16).reshape(2, BLOCK, BLOCK)

        if n + 2 < len(pieces):
            fetches[n + 2].start()

    fetches[0].start()
    fetches[1].start()
    to_near = pltpu.make_async_copy(adjacency_at, adjacency, local_sem.at[0])
    to_near.start()
    place = request(x, z, k, owner, block, mine)
    project(0)
    pl.semaphore_wait(barrier, len(peers))

    started = []

    def send(src, dst, device):
        i = used[0]
        used[0] += 1
        copy = pltpu.make_async_remote_copy(
            src_ref=src,
            dst_ref=dst,
            send_sem=send_sem.at[i],
            recv_sem=recv_sem.at[i],
            device_id=device,
            device_id_type=MESH,
        )
        copy.start()
        started.append(copy)
        return copy

    def arrived(copies):
        for copy in copies:
            copy.wait_recv()

    def piece(i, count):
        return pl.ds(i * (NB // count), NB // count)

    def along_both(up_from, down_from, up_to, down_to, p):
        return [send(up_from.at[p], up_to.at[p], at_z(1)), send(down_from.at[p], down_to.at[p], at_z(-1))]

    quarters = [piece(i, 4) for i in range(4)]
    hop = [along_both(table_one, table_one, up_one, down_one, quarters[0])]
    asks = [send(mine, wanted_all.at[2, me], at_slab(g)) for g in range(1, GROUPS)]
    wanted_all[2, me] = mine[...]
    for i in range(1, 4):
        project(i)
        hop.append(along_both(table_one, table_one, up_one, down_one, quarters[i]))
    to_sources = pltpu.make_async_copy(table_one, sources_one.at[pl.ds(0, NB)], local_sem.at[1])
    to_sources.start()
    arrived(asks)
    asks = [send(wanted_all.at[2], wanted_all.at[2 - s], at_z(s)) for s in (1, -1, 2, -2)]
    sort(count[0], target, source, place, listed, kept)
    to_order = pltpu.make_async_copy(listed, order, local_sem.at[13])
    to_order.start()
    to_keep = pltpu.make_async_copy(kept, keep, local_sem.at[14])
    to_keep.start()
    for i in range(4):
        project(4 + i)
    next_hop = []
    for i in range(2):
        arrived(hop[i])
        next_hop.append(along_both(up_one, down_one, up_two, down_two, quarters[i]))
    arrived(asks)
    to_scalars = pltpu.make_async_copy(wanted_all, wanted, local_sem.at[2])
    to_scalars.start()
    to_scalars.wait()
    to_order.wait()
    to_keep.wait()
    for i in range(2, 4):
        arrived(hop[i])
        next_hop.append(along_both(up_one, down_one, up_two, down_two, quarters[i]))

    def pick(shift, group, step, slot):
        ox, ok = member(x, k, group)
        o = row_of(x, lax.rem(z + step + NZ, NZ), k)
        return jnp.clip(wanted[2 + shift, ox * 2 + ok, 0, 2 * o + slot], 0, NB - 1)

    def pack_share(parts):
        @pl.loop(0, GROUPS)
        def _(g):
            for i, table in parts:
                for slot in range(2):
                    share[g * SHARE + 2 * i + slot] = table[pick(0, g, STEPS[i], slot)]

    def send_share(g, start, size, sources):
        at = g * SHARE + start
        return send(share.at[pl.ds(at, size)], sources.at[pl.ds(NB + at, size)], at_slab(g))

    def pack_relay(up, down):
        @pl.loop(0, GROUPS)
        def _(g):
            for side, (table, sign) in enumerate(((up, 1), (down, -1))):
                for slot in range(2):
                    relay_out[side, g * 2 + slot] = table[pick(sign, g, -2 * sign, slot)]
                relay_out[2 + side, g] = table[pick(2 * sign, g, -2 * sign, side)]

    def send_relay(layer, first):
        near, far = pl.ds(first * 2, 4), pl.ds(first, 2)
        copies = []
        for side, sign in ((0, 1), (1, -1)):
            copies.append(send(relay_out.at[2 + side, far], relay_in.at[layer, 2 + side, far], at_z(2 * sign)))
            copies.append(send(relay_out.at[side, near], relay_in.at[layer, side, near], at_z(sign)))
        return copies

    def pack_far(layer, g):
        at = g * SHARE
        share[at + 10] = relay_in[layer, 0, 2 * g]
        share[at + 11] = relay_in[layer, 0, 2 * g + 1]
        share[at + 12] = relay_in[layer, 1, 2 * g]
        share[at + 13] = relay_in[layer, 1, 2 * g + 1]
        share[at + 14] = relay_in[layer, 2, g]
        share[at + 15] = relay_in[layer, 3, g]

    def forward_far(layer, relays, sources, between):
        copies = []
        for first, then in zip(FIRSTS, between):
            arrived(relays[first])
            for g in (first, first + 1):
                pack_far(layer, g)
                if g > 0:
                    copies.append(send_share(g, 10, 6, sources))
            then()
        return copies

    def keep_own(sources, i):
        copy = pltpu.make_async_copy(
            share.at[pl.ds(0, SHARE)], sources.at[pl.ds(NB, SHARE)], local_sem.at[i]
        )
        copy.start()
        copy.wait()

    def multiply(sources):
        def some(step, total):
            for i in range(UNROLL):
                e = order[0, step * UNROLL + i]
                product = jnp.dot(
                    adjacency[jnp.clip(e & 255, 0, TILES - 1)],
                    sources[jnp.clip(e >> 8, 0, NB + GROUPS * SHARE - 1)],
                    preferred_element_type=jnp.float32,
                )
                total = total * keep[0, step * UNROLL + i] + product
                sums[step * UNROLL + i] = total
            return total

        lax.fori_loop(0, TILES // UNROLL, some, jnp.zeros((BLOCK, BLOCK), jnp.float32))

    def summed(b):
        return sums[jnp.clip(order[1, b], 0, TILES - 1)] * keep[1, b]

    def nothing():
        pass

    others = range(1, GROUPS)

    pack_share([(0, table_one), (1, up_one), (2, down_one)])
    halo_copies = [send_share(g, 0, 6, sources_one) for g in others]
    past = []

    def start_past():
        past.append(along_both(table_past, table_past, up_past, down_past, quarters[len(past)]))

    for i in range(3):
        arrived(next_hop[i])
    start_past()
    arrived(next_hop[3])
    pack_relay(up_two, down_two)
    relays = {first: send_relay(0, first) for first in FIRSTS}
    pack_share([(3, up_two), (4, down_two)])
    halo_copies += [send_share(g, 6, 4, sources_one) for g in others]

    def start_two():
        start_past()
        start_past()

    halo_copies += forward_far(
        0, relays, sources_one, (nothing, start_past, start_two, nothing)
    )
    hop = []
    for i in range(4):
        arrived(past[i])
        hop.append(along_both(up_past, down_past, up_past_two, down_past_two, quarters[i]))
    keep_own(sources_one, 3)
    arrived(halo_copies)
    for copy in halo_copies:
        copy.wait_send()
    pack_share([(0, table_past), (1, up_past), (2, down_past)])
    last_copies = [send_share(g, 0, 6, sources_two) for g in others]
    to_near.wait()
    to_sources.wait()
    multiply(sources_one)

    @pl.loop(0, NB)
    def _(b):
        hidden[b] = jnp.maximum(summed(b) + bias_one[...], 0.0).astype(jnp.bfloat16)

    low, high = piece(0, 2), piece(1, 2)
    from_below = [send(hidden.at[low], near_y.at[0, low], at_y(1))]
    from_above = [send(hidden.at[high], near_y.at[1, high], at_y(-1))]
    from_below.append(send(hidden.at[high], near_y.at[0, high], at_y(1)))
    from_above.append(send(hidden.at[low], near_y.at[1, low], at_y(-1)))

    for copies in relays.values():
        for copy in copies:
            copy.wait_send()
    for copies in hop:
        arrived(copies)
    pack_relay(up_past_two, down_past_two)
    relays_two = {first: send_relay(1, first) for first in FIRSTS}
    pack_share([(3, up_past_two), (4, down_past_two)])
    last_copies += [send_share(g, 6, 4, sources_two) for g in others]
    arrived([from_below[0], from_above[0]])
    across = [
        send(near_y.at[0, low], far_y.at[low], at_y(1)),
        send(near_y.at[1, high], far_y.at[high], at_y(-1)),
    ]

    def part(shift):
        return weight[pl.ds(pl.multiple_of(lax.rem(y + shift, NY) * BLOCK, BLOCK), BLOCK), :]

    def project_hidden():
        arrived([from_below[1], from_above[1], *across])

        @pl.loop(0, NB // 4)
        def _(i):
            here = pl.ds(i * 4, 4)
            total = jnp.zeros((4 * BLOCK, BLOCK), jnp.float32)
            for rows, shift in ((hidden, 0), (near_y.at[0], 3), (near_y.at[1], 1), (far_y, 2)):
                total += jnp.dot(
                    rows[here].reshape(4 * BLOCK, BLOCK),
                    part(shift),
                    preferred_element_type=jnp.float32,
                )
            sources_two[here] = total.astype(jnp.bfloat16).reshape(4, BLOCK, BLOCK)

    last_copies += forward_far(1, relays_two, sources_two, (nothing, nothing, project_hidden, nothing))
    keep_own(sources_two, 4)
    arrived(last_copies)
    multiply(sources_two)

    @pl.loop(0, NB)
    def _(b):
        embedding[b] = (summed(b) + bias_two[...]).astype(jnp.bfloat16)

    waited = halo_copies + [c for copies in relays.values() for c in copies]
    for copy in started:
        if not any(copy is w for w in waited):
            copy.wait_send()


def exchange(count, owner, block, target, source, bias_one, bias_two, weight_one, weight_two, features, history, adjacency):
    def blocks(*count):
        return pltpu.VMEM((*count, BLOCK, BLOCK), jnp.bfloat16)

    table = jax.ShapeDtypeStruct((NB, BLOCK, BLOCK), jnp.bfloat16)
    return pl.pallas_call(
        exchange_kernel,
        out_shape=(table, table),
        in_specs=[SMEM] + [VMEM] * 8 + [ANY] * 3,
        out_specs=(VMEM, VMEM),
        scratch_shapes=[
            pltpu.VMEM((8, 128), jnp.int32),
            pltpu.VMEM((8, 256), jnp.int32),
            pltpu.VMEM((8, 256), jnp.float32),
            pltpu.SMEM((8, 256), jnp.int32),
            pltpu.SMEM((8, 256), jnp.float32),
            pltpu.VMEM((5, GROUPS, 8, 128), jnp.int32),
            pltpu.SMEM((5, GROUPS, 8, 128), jnp.int32),
            pltpu.VMEM((2, NB * BLOCK // 4, 4 * BLOCK), jnp.bfloat16),
            *[blocks(NB)] * 10,
            blocks(4, 2 * GROUPS),
            blocks(2, 4, 2 * GROUPS),
            blocks(GROUPS * SHARE),
            blocks(NB + GROUPS * SHARE),
            blocks(NB + GROUPS * SHARE),
            blocks(TILES),
            pltpu.VMEM((TILES, BLOCK, BLOCK), jnp.float32),
            blocks(2, NB),
            blocks(NB),
            pltpu.SemaphoreType.DMA((COPIES,)),
            pltpu.SemaphoreType.DMA((COPIES,)),
            pltpu.SemaphoreType.DMA((16,)),
        ],
        compiler_params=pltpu.CompilerParams(
            vmem_limit_bytes=60 * 2**20, collective_id=0, has_side_effects=True
        ),
        cost_estimate=pl.CostEstimate(
            flops=2 * 1024 * BLOCK**3, bytes_accessed=32 << 20, transcendentals=0
        ),
        name="exchange",
    )(
        count,
        owner,
        block,
        target,
        source,
        bias_one.reshape(1, BLOCK),
        bias_two.reshape(1, BLOCK),
        weight_one,
        weight_two,
        features,
        history,
        adjacency,
    )


def local(
    features,
    history,
    weight_one,
    weight_two,
    bias_one,
    bias_two,
    adjacency,
    halo_owner,
    halo_block,
    tile_target,
    tile_source,
    tile_count,
):
    hidden, embedding = exchange(
        tile_count,
        halo_owner,
        halo_block,
        tile_target,
        tile_source,
        bias_one,
        bias_two,
        weight_one,
        weight_two,
        features,
        history,
        adjacency,
    )
    return (
        hidden.reshape(NB * BLOCK, BLOCK),
        embedding.reshape(NB * BLOCK, BLOCK),
    )


def solution(mesh):
    return jax.shard_map(
        local,
        mesh=mesh,
        in_specs=(
            P("row", None),
            P("row", None),
            P(None, "col"),
            P(None, "col"),
            P("col"),
            P("col"),
            P("row", None, None),
            P("row", None),
            P("row", None),
            P("row", None),
            P("row", None),
            P("row"),
        ),
        out_specs=(P("row", "col"), P("row", "col")),
        check_vma=False,
    )
```

time: 197 us -> 174 us (0.88)
  waiting for transfers between devices: 9.37 us -> 0 us
  matrix products: 7.9 us -> 0 us
  starting transfers between devices: 6.49 us -> 0 us
  Pallas kernels: 163 us -> 168 us
    ppermute x2 -> x0, waiting for transfers between devices: 9.37 us -> none  [the longest x1 6.28 us: local(): down_one = lax.ppermute(table_one, 'row', along_z(-1))]
    dot_general x2 -> x0, matrix products: 7.9 us -> none  [project(): jnp.dot(rows, weight, preferred_element_type=jnp.float32)]
    ppermute x2 -> x0, starting transfers between devices: 6.49 us -> none  [the longest x1 6.49 us: local(): down_one = lax.ppermute(table_one, 'row', along_z(-1))]
    pallas_call x3 -> x1, Pallas kernels: 163 us -> 168 us  [exchange(): pl.pallas_call(exchange_kernel, out_shape=(table, table), in_specs=[SMEM]...]
    unnamed x12 -> x2, local copies, waits for them, and re-layouts: 6.39 us -> 4.52 us
  transfers between devices with their start and end apart: 2 -> 0, of which waited for: 2 -> 0; matrix products, arithmetic and copies ran while one was open for 3% -> 0% of each run, Pallas kernels for 5% -> 0%
where the time goes in v3:
time: 174 us; the launch traced here: 173 us
  Pallas kernels  168 us (97%)
  local copies, waits for them, and re-layouts  4.52 us (3%)
    pallas_call x1, Pallas kernels, exchange(): pl.pallas_call(exchange_kernel, out_shape=(table, table), in_specs=[SMEM]...  168 us
    unnamed x2, local copies, waits for them, and re-layouts  4.52 us

profile of v3, /device:TPU:1, one launch (start us, length us, event | category | flops | bytes accessed | tf_op | source)
XLA Modules:
  0.0 173.4 jit_solution(448392135656937818)
XLA Ops:
  1.3 167.6 %exchange.1 = (bf16[32,128,128]{2,1,0:T(8,128)(2,1)}, bf16[32,128,128]{2,1,0:T(8,128)(2,1)}) custom-call(s32[1]{0:T(128)S(6)} %copy.16.count, s32[1,96]{1,0:T(1,128)} %owner.1, s32[1,96]{1,0:T(1,128)} %block.1, s32[1,192]{1,0:T(1,128)} %target.1, s32[1,192]{1,0:T(1,128)} %source.1, f32[1,128]{1,0:T(1,128)} %bitcast.6, f32[1,128]{1,0:T(1,128)} %bitcast.7, ...), custom_call_target="tpu_custom_call" | custom-call | flops 4294967296 | bytes 33554432 | tf_op jit(solution)/shard_map/exchange/pallas_call | solution.py:433
  168.9 2.3 %copy.17 = bf16[4096,128]{1,0:T(8,128)(2,1)} copy(bf16[4096,128]{1,0:T(8,128)(2,1)} %bitcast.5) | data formatting | bytes 2097152
  171.1 2.3 %copy.18 = bf16[4096,128]{1,0:T(8,128)(2,1)} copy(bf16[4096,128]{1,0:T(8,128)(2,1)} %bitcast.4) | data formatting | bytes 2097152

commit v4 on v3

--- a/solution.py
+++ b/solution.py
@@ -88,22 +88,30 @@
     kept[1:2, 0:128] = jnp.where(many > 0, 1.0, 0.0)
 
 
-COPIES = 128
+COPIES = 106
 
 
 def exchange_kernel(
     count,
+    owner_at,
+    block_at,
+    target_at,
+    source_at,
+    bias_at,
+    first_weight_at,
+    weight_at,
+    features,
+    history,
+    adjacency_at,
+    hidden_at,
+    embedding_at,
     owner,
     block,
     target,
     source,
     bias_one,
-    bias_two,
     first_weight,
     weight,
-    features,
-    history,
-    adjacency_at,
     hidden,
     embedding,
     mine,
@@ -161,6 +169,23 @@
     for peer in peers:
         pl.semaphore_signal(barrier, inc=1, device_id=peer, device_id_type=MESH)
 
+    small = [
+        pltpu.make_async_copy(at, here, local_sem.at[16 + i])
+        for i, (at, here) in enumerate(
+            (
+                (first_weight_at, first_weight),
+                (owner_at, owner),
+                (block_at, block),
+                (target_at, target),
+                (source_at, source),
+                (bias_at, bias_one),
+                (weight_at, weight),
+            )
+        )
+    ]
+    for copy in small[:3]:
+        copy.start()
+
     rows = NB * BLOCK // 4
     pieces = [(table, w, at, i) for table, w, at in ((table_one, first_weight, features), (table_past, weight, history)) for i in range(4)]
     fetches = [
@@ -183,8 +208,12 @@
 
     fetches[0].start()
     fetches[1].start()
+    for copy in small[3:]:
+        copy.start()
     to_near = pltpu.make_async_copy(adjacency_at, adjacency, local_sem.at[0])
     to_near.start()
+    for copy in small:
+        copy.wait()
     place = request(x, z, k, owner, block, mine)
     project(0)
     pl.semaphore_wait(barrier, len(peers))
@@ -217,16 +246,19 @@
         return [send(up_from.at[p], up_to.at[p], at_z(1)), send(down_from.at[p], down_to.at[p], at_z(-1))]
 
     quarters = [piece(i, 4) for i in range(4)]
+    halves = [piece(i, 2) for i in range(2)]
     hop = [along_both(table_one, table_one, up_one, down_one, quarters[0])]
     asks = [send(mine, wanted_all.at[2, me], at_slab(g)) for g in range(1, GROUPS)]
     wanted_all[2, me] = mine[...]
-    for i in range(1, 4):
-        project(i)
-        hop.append(along_both(table_one, table_one, up_one, down_one, quarters[i]))
+    project(1)
+    hop.append(along_both(table_one, table_one, up_one, down_one, quarters[1]))
+    arrived(asks)
+    asks = [send(wanted_all.at[2], wanted_all.at[2 - s], at_z(s)) for s in (1, -1, 2, -2)]
+    project(2)
+    project(3)
+    hop.append(along_both(table_one, table_one, up_one, down_one, halves[1]))
     to_sources = pltpu.make_async_copy(table_one, sources_one.at[pl.ds(0, NB)], local_sem.at[1])
     to_sources.start()
-    arrived(asks)
-    asks = [send(wanted_all.at[2], wanted_all.at[2 - s], at_z(s)) for s in (1, -1, 2, -2)]
     sort(count[0], target, source, place, listed, kept)
     to_order = pltpu.make_async_copy(listed, order, local_sem.at[13])
     to_order.start()
@@ -237,16 +269,15 @@
     next_hop = []
     for i in range(2):
         arrived(hop[i])
-        next_hop.append(along_both(up_one, down_one, up_two, down_two, quarters[i]))
+    next_hop.append(along_both(up_one, down_one, up_two, down_two, halves[0]))
     arrived(asks)
     to_scalars = pltpu.make_async_copy(wanted_all, wanted, local_sem.at[2])
     to_scalars.start()
     to_scalars.wait()
     to_order.wait()
     to_keep.wait()
-    for i in range(2, 4):
-        arrived(hop[i])
-        next_hop.append(along_both(up_one, down_one, up_two, down_two, quarters[i]))
+    arrived(hop[2])
+    next_hop.append(along_both(up_one, down_one, up_two, down_two, halves[1]))
 
     def pick(shift, group, step, slot):
         ox, ok = member(x, k, group)
@@ -331,20 +362,18 @@
     others = range(1, GROUPS)
 
     pack_share([(0, table_one), (1, up_one), (2, down_one)])
-    halo_copies = [send_share(g, 0, 6, sources_one) for g in others]
     past = []
 
     def start_past():
         past.append(along_both(table_past, table_past, up_past, down_past, quarters[len(past)]))
 
-    for i in range(3):
-        arrived(next_hop[i])
+    arrived(next_hop[0])
     start_past()
-    arrived(next_hop[3])
+    arrived(next_hop[1])
     pack_relay(up_two, down_two)
     relays = {first: send_relay(0, first) for first in FIRSTS}
     pack_share([(3, up_two), (4, down_two)])
-    halo_copies += [send_share(g, 6, 4, sources_one) for g in others]
+    halo_copies = [send_share(g, 0, 10, sources_one) for g in others]
 
     def start_two():
         start_past()
@@ -354,9 +383,9 @@
         0, relays, sources_one, (nothing, start_past, start_two, nothing)
     )
     hop = []
-    for i in range(4):
-        arrived(past[i])
-        hop.append(along_both(up_past, down_past, up_past_two, down_past_two, quarters[i]))
+    for i in range(2):
+        arrived(past[2 * i] + past[2 * i + 1])
+        hop.append(along_both(up_past, down_past, up_past_two, down_past_two, halves[i]))
     keep_own(sources_one, 3)
     arrived(halo_copies)
     for copy in halo_copies:
@@ -371,6 +400,8 @@
     def _(b):
         hidden[b] = jnp.maximum(summed(b) + bias_one[...], 0.0).astype(jnp.bfloat16)
 
+    hidden_out = pltpu.make_async_copy(hidden, hidden_at, local_sem.at[15])
+    hidden_out.start()
     low, high = piece(0, 2), piece(1, 2)
     from_below = [send(hidden.at[low], near_y.at[0, low], at_y(1))]
     from_above = [send(hidden.at[high], near_y.at[1, high], at_y(-1))]
@@ -415,27 +446,49 @@
     arrived(last_copies)
     multiply(sources_two)
 
-    @pl.loop(0, NB)
-    def _(b):
-        embedding[b] = (summed(b) + bias_two[...]).astype(jnp.bfloat16)
-
+    outs = []
+    for i in range(4):
+
+        @pl.loop(i * NB // 4, (i + 1) * NB // 4)
+        def _(b):
+            embedding[b] = summed(b)
+
+        outs.append(
+            pltpu.make_async_copy(embedding.at[quarters[i]], embedding_at.at[quarters[i]], local_sem.at[24 + i])
+        )
+        outs[i].start()
+    hidden_out.wait()
+    for copy in outs:
+        copy.wait()
+    assert used[0] == COPIES
     waited = halo_copies + [c for copies in relays.values() for c in copies]
     for copy in started:
         if not any(copy is w for w in waited):
             copy.wait_send()
 
 
-def exchange(count, owner, block, target, source, bias_one, bias_two, weight_one, weight_two, features, history, adjacency):
+def exchange(count, owner, block, target, source, bias, weight_one, weight_two, features, history, adjacency):
     def blocks(*count):
         return pltpu.VMEM((*count, BLOCK, BLOCK), jnp.bfloat16)
 
-    table = jax.ShapeDtypeStruct((NB, BLOCK, BLOCK), jnp.bfloat16)
     return pl.pallas_call(
         exchange_kernel,
-        out_shape=(table, table),
-        in_specs=[SMEM] + [VMEM] * 8 + [ANY] * 3,
-        out_specs=(VMEM, VMEM),
+        out_shape=(
+            jax.ShapeDtypeStruct((NB, BLOCK, BLOCK), jnp.bfloat16),
+            jax.ShapeDtypeStruct((NB, BLOCK, BLOCK), jnp.float32),
+        ),
+        in_specs=[SMEM] + [ANY] * 10,
+        out_specs=(ANY, ANY),
         scratch_shapes=[
+            pltpu.VMEM((1, HALO), jnp.int32),
+            pltpu.VMEM((1, HALO), jnp.int32),
+            pltpu.VMEM((1, TILES), jnp.int32),
+            pltpu.VMEM((1, TILES), jnp.int32),
+            pltpu.VMEM((1, BLOCK), jnp.float32),
+            pltpu.VMEM((4 * BLOCK, BLOCK), jnp.bfloat16),
+            pltpu.VMEM((4 * BLOCK, BLOCK), jnp.bfloat16),
+            blocks(NB),
+            pltpu.VMEM((NB, BLOCK, BLOCK), jnp.float32),
             pltpu.VMEM((8, 128), jnp.int32),
             pltpu.VMEM((8, 256), jnp.int32),
             pltpu.VMEM((8, 256), jnp.float32),
@@ -456,7 +509,7 @@
             blocks(NB),
             pltpu.SemaphoreType.DMA((COPIES,)),
             pltpu.SemaphoreType.DMA((COPIES,)),
-            pltpu.SemaphoreType.DMA((16,)),
+            pltpu.SemaphoreType.DMA((28,)),
         ],
         compiler_params=pltpu.CompilerParams(
             vmem_limit_bytes=60 * 2**20, collective_id=0, has_side_effects=True
@@ -471,8 +524,7 @@
         block,
         target,
         source,
-        bias_one.reshape(1, BLOCK),
-        bias_two.reshape(1, BLOCK),
+        bias.reshape(1, BLOCK),
         weight_one,
         weight_two,
         features,
@@ -495,24 +547,22 @@
     tile_source,
     tile_count,
 ):
-    hidden, embedding = exchange(
+    hidden, summed = exchange(
         tile_count,
         halo_owner,
         halo_block,
         tile_target,
         tile_source,
         bias_one,
-        bias_two,
         weight_one,
         weight_two,
         features,
         history,
         adjacency,
     )
-    return (
-        hidden.reshape(NB * BLOCK, BLOCK),
-        embedding.reshape(NB * BLOCK, BLOCK),
-    )
+    hidden = jnp.maximum(hidden.reshape(NB * BLOCK, BLOCK), 0)
+    embedding = (summed.reshape(NB * BLOCK, BLOCK) + bias_two).astype(jnp.bfloat16)
+    return (hidden, embedding)
 
 
 def solution(mesh):

time: 174 us -> 171 us (0.983)
  local copies, waits for them, and re-layouts: 4.52 us -> 0.01 us
  other arithmetic: 0 us -> 3.49 us
  Pallas kernels: 168 us -> 166 us
    unnamed x2 -> x4, local copies, waits for them, and re-layouts: 4.52 us -> 0.01 us
    max x0 -> x1, other arithmetic: none -> 2.41 us  [local(): hidden = jnp.maximum(hidden.reshape(NB * BLOCK, BLOCK), 0)]
where the time goes in v4:
time: 171 us
  Pallas kernels  166 us (97%)
  other arithmetic  3.49 us (2%)
    pallas_call x1, Pallas kernels, exchange(): pl.pallas_call(exchange_kernel, out_shape=(jax.ShapeDtypeStruct((NB, BLOC...  166 us

profile of v4, /device:TPU:1, one launch (start us, length us, event | category | flops | bytes accessed | tf_op | source)
XLA Modules:
  0.0 170.8 jit_solution(15873527850118165552)
XLA Ops:
  1.3 166.0 %exchange.1 = (bf16[32,128,128]{2,1,0:T(8,128)(2,1)}, f32[32,128,128]{2,1,0:T(8,128)}) custom-call(s32[1]{0:T(128)S(6)} %copy.14.count, s32[1,96]{1,0:T(1,128)} %owner_at.1, s32[1,96]{1,0:T(1,128)} %block_at.1, s32[1,192]{1,0:T(1,128)} %target_at.1, s32[1,192]{1,0:T(1,128)} %source_at.1, f32[1,128]{1,0:T(1,128)} %bitcast.7, ...), custom_call_target="tpu_custom_call" | custom-call | flops 4294967296 | bytes 33554432 | tf_op jit(solution)/shard_map/exchange/pallas_call | solution.py:474
  167.3 0.0 copy-start
  167.3 0.0 copy-start.1
  167.3 2.4 %broadcast_maximum_fusion = bf16[32,128,128]{2,1,0:T(8,128)(2,1)} fusion(bf16[32,128,128]{2,1,0:T(8,128)(2,1)} %get-tuple-element.4), kind=kLoop, calls=%fused_computation.2 | loop fusion | flops 524288 | bytes 2097152 | tf_op jit(solution)/shard_map/max | solution.py:563
  169.7 0.0 copy-done
  169.7 0.0 copy-done.1
  169.7 1.1 fusion
Async XLA Ops:
  167.3 2.4 %copy-start = (f32[32,128,128]{2,1,0:T(8,128)S(1)}, f32[32,128,128]{2,1,0:T(8,128)}, u32[]{:S(2)}) copy-start(f32[32,128,128]{2,1,0:T(8,128)} %get-tuple-element.5) | copy-start | bytes 6291460
  167.3 2.4 %copy-start.1 = (f32[128]{0:T(128)S(1)}, f32[128]{0:T(128)}, u32[]{:S(2)}) copy-start(f32[128]{0:T(128)} %param.17) | copy-start | bytes 1540

commit v5 on v4

--- a/solution.py
+++ b/solution.py
@@ -12,6 +12,7 @@
 NX, NZ, NY = 4, 8, 4
 GROUPS = 8
 SHARE = 16
+PAIRS = (TILES + NB) // 2
 UNROLL = 8
 FIRSTS = (4, 2, 6, 0)
 MESH = pl.DeviceIdType.MESH
@@ -64,8 +65,7 @@
 
 
 def sort(live, target, source, place, listed, kept):
-    line, square = (1, TILES), (TILES, TILES)
-    ids = lane(line, 1)
+    ids = lane((1, TILES), 1)
     s = source[...]
     slots = lane((HALO, TILES), 0)
     halo = jnp.sum(jnp.where(slots == s - NB, place, 0), axis=0, keepdims=True)
@@ -75,16 +75,23 @@
     goal = upright(row)
     key = row * 256 + ids
     rank = jnp.sum(jnp.where(key < upright(key), 1, 0), axis=1, keepdims=True)
-    here = rank == lane(square, 1)
+    before = jnp.sum(jnp.where(row < goal, 1, 0), axis=1, keepdims=True)
+    mine = goal == lane((TILES, 128), 1)
+    many = jnp.sum(jnp.where(mine, 1, 0), axis=0, keepdims=True)
+    pairs = (many + 1) >> 1
+    square = (128, 128)
+    start = jnp.sum(
+        jnp.where(lane(square, 0) < lane(square, 1), upright(pairs), 0), axis=0, keepdims=True
+    )
+    spot = 2 * jnp.sum(jnp.where(mine, start, 0), axis=1, keepdims=True) + rank - before
+    here = spot == lane((TILES, 256), 1)
+    filled = jnp.sum(jnp.where(here, 1, 0), axis=0, keepdims=True)
     order = jnp.sum(jnp.where(here, entry, 0), axis=0, keepdims=True)
-    goals = jnp.sum(jnp.where(here, goal, 0), axis=0, keepdims=True)
-    before = jnp.sum(jnp.where(goal < goals, 1, 0), axis=0, keepdims=True)
-    listed[0:1, 0:TILES] = order
-    kept[0:1, 0:TILES] = jnp.where(before == ids, 0.0, 1.0)
-    blocks = lane((TILES, 128), 1)
-    upto = jnp.sum(jnp.where(goal <= blocks, 1, 0), axis=0, keepdims=True)
-    many = jnp.sum(jnp.where(goal == blocks, 1, 0), axis=0, keepdims=True)
-    listed[1:2, 0:128] = jnp.maximum(upto - 1, 0)
+    listed[0:1, 0:256] = jnp.where(filled > 0, order, TILES)
+    opens = (upright(start) == lane(square, 1)) & (upright(many) > 0)
+    first = jnp.sum(jnp.where(opens, 1, 0), axis=0, keepdims=True)
+    kept[0:1, 0:128] = jnp.where(first > 0, 0.0, 1.0)
+    listed[1:2, 0:128] = jnp.maximum(start + pairs - 1, 0)
     kept[1:2, 0:128] = jnp.where(many > 0, 1.0, 0.0)
 
 
@@ -210,8 +217,9 @@
     fetches[1].start()
     for copy in small[3:]:
         copy.start()
-    to_near = pltpu.make_async_copy(adjacency_at, adjacency, local_sem.at[0])
+    to_near = pltpu.make_async_copy(adjacency_at, adjacency.at[pl.ds(0, TILES)], local_sem.at[0])
     to_near.start()
+    adjacency[TILES] = jnp.zeros((BLOCK, BLOCK), jnp.bfloat16)
     for copy in small:
         copy.wait()
     place = request(x, z, k, owner, block, mine)
@@ -284,8 +292,8 @@
         o = row_of(x, lax.rem(z + step + NZ, NZ), k)
         return jnp.clip(wanted[2 + shift, ox * 2 + ok, 0, 2 * o + slot], 0, NB - 1)
 
-    def pack_share(parts):
-        @pl.loop(0, GROUPS)
+    def pack_share(parts, first=None):
+        @pl.loop(0 if first is None else first, GROUPS if first is None else first + 2)
         def _(g):
             for i, table in parts:
                 for slot in range(2):
@@ -295,8 +303,8 @@
         at = g * SHARE + start
         return send(share.at[pl.ds(at, size)], sources.at[pl.ds(NB + at, size)], at_slab(g))
 
-    def pack_relay(up, down):
-        @pl.loop(0, GROUPS)
+    def pack_relay(up, down, first):
+        @pl.loop(first, first + 2)
         def _(g):
             for side, (table, sign) in enumerate(((up, 1), (down, -1))):
                 for slot in range(2):
@@ -339,22 +347,29 @@
         copy.wait()
 
     def multiply(sources):
+        def tile(e):
+            return adjacency[jnp.clip(e & 255, 0, TILES)]
+
+        def origin(e):
+            return sources[jnp.clip(e >> 8, 0, NB + GROUPS * SHARE - 1)]
+
         def some(step, total):
             for i in range(UNROLL):
-                e = order[0, step * UNROLL + i]
+                pair = step * UNROLL + i
+                one, two = order[0, 2 * pair], order[0, 2 * pair + 1]
                 product = jnp.dot(
-                    adjacency[jnp.clip(e & 255, 0, TILES - 1)],
-                    sources[jnp.clip(e >> 8, 0, NB + GROUPS * SHARE - 1)],
+                    jnp.concatenate([tile(one), tile(two)], axis=1),
+                    jnp.concatenate([origin(one), origin(two)], axis=0),
                     preferred_element_type=jnp.float32,
                 )
-                total = total * keep[0, step * UNROLL + i] + product
-                sums[step * UNROLL + i] = total
+                total = total * keep[0, pair] + product
+                sums[pair] = total
             return total
 
-        lax.fori_loop(0, TILES // UNROLL, some, jnp.zeros((BLOCK, BLOCK), jnp.float32))
+        lax.fori_loop(0, PAIRS // UNROLL, some, jnp.zeros((BLOCK, BLOCK), jnp.float32))
 
     def summed(b):
-        return sums[jnp.clip(order[1, b], 0, TILES - 1)] * keep[1, b]
+        return sums[jnp.clip(order[1, b], 0, PAIRS - 1)] * keep[1, b]
 
     def nothing():
         pass
@@ -370,8 +385,10 @@
     arrived(next_hop[0])
     start_past()
     arrived(next_hop[1])
-    pack_relay(up_two, down_two)
-    relays = {first: send_relay(0, first) for first in FIRSTS}
+    relays = {}
+    for first in FIRSTS:
+        pack_relay(up_two, down_two, first)
+        relays[first] = send_relay(0, first)
     pack_share([(3, up_two), (4, down_two)])
     halo_copies = [send_share(g, 0, 10, sources_one) for g in others]
 
@@ -413,10 +430,14 @@
             copy.wait_send()
     for copies in hop:
         arrived(copies)
-    pack_relay(up_past_two, down_past_two)
-    relays_two = {first: send_relay(1, first) for first in FIRSTS}
-    pack_share([(3, up_past_two), (4, down_past_two)])
-    last_copies += [send_share(g, 6, 4, sources_two) for g in others]
+    relays_two = {}
+    for first in FIRSTS:
+        pack_relay(up_past_two, down_past_two, first)
+        relays_two[first] = send_relay(1, first)
+        pack_share([(3, up_past_two), (4, down_past_two)], first)
+        for g in (first, first + 1):
+            if g > 0:
+                last_copies.append(send_share(g, 6, 4, sources_two))
     arrived([from_below[0], from_above[0]])
     across = [
         send(near_y.at[0, low], far_y.at[low], at_y(1)),
@@ -503,8 +524,8 @@
             blocks(GROUPS * SHARE),
             blocks(NB + GROUPS * SHARE),
             blocks(NB + GROUPS * SHARE),
-            blocks(TILES),
-            pltpu.VMEM((TILES, BLOCK, BLOCK), jnp.float32),
+            blocks(TILES + 1),
+            pltpu.VMEM((PAIRS, BLOCK, BLOCK), jnp.float32),
             blocks(2, NB),
             blocks(NB),
             pltpu.SemaphoreType.DMA((COPIES,)),
@@ -531,6 +552,50 @@
         history,
         adjacency,
     )
+
+
+def finish_kernel(hidden_at, summed_at, bias_at, hidden, embedding, summed, value, bias, sem):
+    across = pltpu.make_async_copy(hidden_at, hidden, sem.at[0])
+    take = pltpu.make_async_copy(bias_at, bias, sem.at[1])
+    width = NB // 4
+    parts = [pl.ds(i * width, width) for i in range(4)]
+    ins = [pltpu.make_async_copy(summed_at.at[p], summed.at[p], sem.at[2 + i]) for i, p in enumerate(parts)]
+    outs = [pltpu.make_async_copy(value.at[p], embedding.at[p], sem.at[6 + i]) for i, p in enumerate(parts)]
+    take.start()
+    for copy in ins:
+        copy.start()
+    across.start()
+    take.wait()
+    for i in range(4):
+        ins[i].wait()
+
+        @pl.loop(i * width, (i + 1) * width, unroll=2)
+        def _(b):
+            value[b] = (summed[b] + bias[...]).astype(jnp.bfloat16)
+
+        outs[i].start()
+    for copy in outs:
+        copy.wait()
+    across.wait()
+
+
+def finish(hidden, summed, bias):
+    table = jax.ShapeDtypeStruct((NB, BLOCK, BLOCK), jnp.bfloat16)
+    return pl.pallas_call(
+        finish_kernel,
+        out_shape=(table, table),
+        in_specs=[ANY] * 3,
+        out_specs=(ANY, ANY),
+        scratch_shapes=[
+            pltpu.VMEM((NB, BLOCK, BLOCK), jnp.float32),
+            pltpu.VMEM((NB, BLOCK, BLOCK), jnp.bfloat16),
+            pltpu.VMEM((1, BLOCK), jnp.float32),
+            pltpu.SemaphoreType.DMA((10,)),
+        ],
+        compiler_params=pltpu.CompilerParams(vmem_limit_bytes=60 * 2**20),
+        cost_estimate=pl.CostEstimate(flops=0, bytes_accessed=6 << 20, transcendentals=0),
+        name="finish",
+    )(hidden, summed, bias.reshape(1, BLOCK))
 
 
 def local(
@@ -560,9 +625,11 @@
         history,
         adjacency,
     )
-    hidden = jnp.maximum(hidden.reshape(NB * BLOCK, BLOCK), 0)
-    embedding = (summed.reshape(NB * BLOCK, BLOCK) + bias_two).astype(jnp.bfloat16)
-    return (hidden, embedding)
+    hidden, embedding = finish(hidden, summed, bias_two)
+    return (
+        hidden.reshape(NB * BLOCK, BLOCK),
+        embedding.reshape(NB * BLOCK, BLOCK),
+    )
 
 
 def solution(mesh):

time: 171 us -> 198 us (1.16)
  Pallas kernels: 166 us -> 197 us
  other arithmetic: 3.49 us -> 0 us
    pallas_call x0 -> x1, Pallas kernels: none -> 33 us  [finish(): pl.pallas_call(finish_kernel, out_shape=(table, table), in_specs=[ANY] *...]
    max x1 -> x0, other arithmetic: 2.41 us -> none  [local(): hidden = jnp.maximum(hidden.reshape(NB * BLOCK, BLOCK), 0)]
    pallas_call x1, Pallas kernels: 166 us -> 164 us  [exchange(): pl.pallas_call(exchange_kernel, out_shape=(jax.ShapeDtypeStruct((NB, BLOC...]
where the time goes in v5:
time: 198 us
  Pallas kernels  197 us (99%)
    pallas_call x1, Pallas kernels, exchange(): pl.pallas_call(exchange_kernel, out_shape=(jax.ShapeDtypeStruct((NB, BLOC...  164 us
    pallas_call x1, Pallas kernels, finish(): pl.pallas_call(finish_kernel, out_shape=(table, table), in_specs=[ANY] *...  33 us

profile of v5, /device:TPU:1, one launch (start us, length us, event | category | flops | bytes accessed | tf_op | source)
XLA Modules:
  0.0 198.1 jit_solution(14416614839818403886)
XLA Ops:
  1.3 163.8 %exchange.1 = (bf16[32,128,128]{2,1,0:T(8,128)(2,1)}, f32[32,128,128]{2,1,0:T(8,128)}) custom-call(s32[1]{0:T(128)S(6)} %copy.14.count, s32[1,96]{1,0:T(1,128)} %owner_at.1, s32[1,96]{1,0:T(1,128)} %block_at.1, s32[1,192]{1,0:T(1,128)} %target_at.1, s32[1,192]{1,0:T(1,128)} %source_at.1, f32[1,128]{1,0:T(1,128)} %bitcast.7, ...), custom_call_target="tpu_custom_call" | custom-call | flops 4294967296 | bytes 33554432 | tf_op jit(solution)/shard_map/exchange/pallas_call | solution.py:495
  165.1 33.0 %finish.1 = (bf16[32,128,128]{2,1,0:T(8,128)(2,1)}, bf16[32,128,128]{2,1,0:T(8,128)(2,1)}) custom-call(bf16[32,128,128]{2,1,0:T(8,128)(2,1)} %get-tuple-element.6.hidden_at, f32[32,128,128]{2,1,0:T(8,128)} %get-tuple-element.7.summed_at, f32[1,128]{1,0:T(1,128)} %bitcast.4), custom_call_target="tpu_custom_call" | custom-call | bytes 6291456 | tf_op jit(solution)/shard_map/finish/pallas_call | solution.py:584

commit v6 on v5

--- a/solution.py
+++ b/solution.py
@@ -104,7 +104,8 @@
     block_at,
     target_at,
     source_at,
-    bias_at,
+    bias_one_at,
+    bias_two_at,
     first_weight_at,
     weight_at,
     features,
@@ -117,6 +118,7 @@
     target,
     source,
     bias_one,
+    bias_two,
     first_weight,
     weight,
     hidden,
@@ -185,7 +187,8 @@
                 (block_at, block),
                 (target_at, target),
                 (source_at, source),
-                (bias_at, bias_one),
+                (bias_one_at, bias_one),
+                (bias_two_at, bias_two),
                 (weight_at, weight),
             )
         )
@@ -472,7 +475,7 @@
 
         @pl.loop(i * NB // 4, (i + 1) * NB // 4)
         def _(b):
-            embedding[b] = summed(b)
+            embedding[b] = (summed(b) + bias_two[...]).astype(jnp.bfloat16)
 
         outs.append(
             pltpu.make_async_copy(embedding.at[quarters[i]], embedding_at.at[quarters[i]], local_sem.at[24 + i])
@@ -488,17 +491,14 @@
             copy.wait_send()
 
 
-def exchange(count, owner, block, target, source, bias, weight_one, weight_two, features, history, adjacency):
+def exchange(count, owner, block, target, source, bias_one, bias_two, weight_one, weight_two, features, history, adjacency):
     def blocks(*count):
         return pltpu.VMEM((*count, BLOCK, BLOCK), jnp.bfloat16)
 
     return pl.pallas_call(
         exchange_kernel,
-        out_shape=(
-            jax.ShapeDtypeStruct((NB, BLOCK, BLOCK), jnp.bfloat16),
-            jax.ShapeDtypeStruct((NB, BLOCK, BLOCK), jnp.float32),
-        ),
-        in_specs=[SMEM] + [ANY] * 10,
+        out_shape=(jax.ShapeDtypeStruct((NB, BLOCK, BLOCK), jnp.bfloat16),) * 2,
+        in_specs=[SMEM] + [ANY] * 11,
         out_specs=(ANY, ANY),
         scratch_shapes=[
             pltpu.VMEM((1, HALO), jnp.int32),
@@ -506,10 +506,11 @@
             pltpu.VMEM((1, TILES), jnp.int32),
             pltpu.VMEM((1, TILES), jnp.int32),
             pltpu.VMEM((1, BLOCK), jnp.float32),
+            pltpu.VMEM((1, BLOCK), jnp.float32),
             pltpu.VMEM((4 * BLOCK, BLOCK), jnp.bfloat16),
             pltpu.VMEM((4 * BLOCK, BLOCK), jnp.bfloat16),
             blocks(NB),
-            pltpu.VMEM((NB, BLOCK, BLOCK), jnp.float32),
+            blocks(NB),
             pltpu.VMEM((8, 128), jnp.int32),
             pltpu.VMEM((8, 256), jnp.int32),
             pltpu.VMEM((8, 256), jnp.float32),
@@ -545,7 +546,8 @@
         block,
         target,
         source,
-        bias.reshape(1, BLOCK),
+        bias_one.reshape(1, BLOCK),
+        bias_two.reshape(1, BLOCK),
         weight_one,
         weight_two,
         features,
@@ -554,48 +556,38 @@
     )
 
 
-def finish_kernel(hidden_at, summed_at, bias_at, hidden, embedding, summed, value, bias, sem):
-    across = pltpu.make_async_copy(hidden_at, hidden, sem.at[0])
-    take = pltpu.make_async_copy(bias_at, bias, sem.at[1])
-    width = NB // 4
-    parts = [pl.ds(i * width, width) for i in range(4)]
-    ins = [pltpu.make_async_copy(summed_at.at[p], summed.at[p], sem.at[2 + i]) for i, p in enumerate(parts)]
-    outs = [pltpu.make_async_copy(value.at[p], embedding.at[p], sem.at[6 + i]) for i, p in enumerate(parts)]
-    take.start()
+def finish_kernel(hidden_at, embedding_at, hidden, embedding, held, sem):
+    ins, outs = [], []
+    for i, (at, to) in enumerate(((hidden_at, hidden), (embedding_at, embedding))):
+        for j in range(2):
+            part = pl.ds(j * (NB // 2), NB // 2)
+            n = 2 * i + j
+            ins.append(pltpu.make_async_copy(at.at[part], held.at[n], sem.at[n]))
+            outs.append(pltpu.make_async_copy(held.at[n], to.at[part], sem.at[4 + n]))
     for copy in ins:
         copy.start()
-    across.start()
-    take.wait()
-    for i in range(4):
-        ins[i].wait()
-
-        @pl.loop(i * width, (i + 1) * width, unroll=2)
-        def _(b):
-            value[b] = (summed[b] + bias[...]).astype(jnp.bfloat16)
-
-        outs[i].start()
+    for come, go in zip(ins, outs):
+        come.wait()
+        go.start()
     for copy in outs:
         copy.wait()
-    across.wait()
-
-
-def finish(hidden, summed, bias):
+
+
+def finish(hidden, embedding):
     table = jax.ShapeDtypeStruct((NB, BLOCK, BLOCK), jnp.bfloat16)
     return pl.pallas_call(
         finish_kernel,
         out_shape=(table, table),
-        in_specs=[ANY] * 3,
+        in_specs=[ANY] * 2,
         out_specs=(ANY, ANY),
         scratch_shapes=[
-            pltpu.VMEM((NB, BLOCK, BLOCK), jnp.float32),
-            pltpu.VMEM((NB, BLOCK, BLOCK), jnp.bfloat16),
-            pltpu.VMEM((1, BLOCK), jnp.float32),
-            pltpu.SemaphoreType.DMA((10,)),
+            pltpu.VMEM((4, NB // 2, BLOCK, BLOCK), jnp.bfloat16),
+            pltpu.SemaphoreType.DMA((8,)),
         ],
         compiler_params=pltpu.CompilerParams(vmem_limit_bytes=60 * 2**20),
-        cost_estimate=pl.CostEstimate(flops=0, bytes_accessed=6 << 20, transcendentals=0),
+        cost_estimate=pl.CostEstimate(flops=0, bytes_accessed=4 << 20, transcendentals=0),
         name="finish",
-    )(hidden, summed, bias.reshape(1, BLOCK))
+    )(hidden, embedding)
 
 
 def local(
@@ -612,20 +604,21 @@
     tile_source,
     tile_count,
 ):
-    hidden, summed = exchange(
+    hidden, embedding = exchange(
         tile_count,
         halo_owner,
         halo_block,
         tile_target,
         tile_source,
         bias_one,
+        bias_two,
         weight_one,
         weight_two,
         features,
         history,
         adjacency,
     )
-    hidden, embedding = finish(hidden, summed, bias_two)
+    hidden, embedding = finish(hidden, embedding)
     return (
         hidden.reshape(NB * BLOCK, BLOCK),
         embedding.reshape(NB * BLOCK, BLOCK),

time: 198 us -> 168 us (0.85)
  Pallas kernels: 197 us -> 166 us
    pallas_call x1, Pallas kernels: 33 us -> 2.42 us  [finish(): pl.pallas_call(finish_kernel, out_shape=(table, table), in_specs=[ANY] *...]
where the time goes in v6:
time: 168 us; the launch traced here: 167 us
  Pallas kernels  166 us (99%)
    pallas_call x1, Pallas kernels, exchange(): pl.pallas_call(exchange_kernel, out_shape=(jax.ShapeDtypeStruct((NB, BLOC...  164 us

profile of v6, /device:TPU:1, one launch (start us, length us, event | category | flops | bytes accessed | tf_op | source)
XLA Modules:
  0.0 167.4 jit_solution(9033372652693774700)
XLA Ops:
  1.3 163.7 %exchange.1 = (bf16[32,128,128]{2,1,0:T(8,128)(2,1)}, bf16[32,128,128]{2,1,0:T(8,128)(2,1)}) custom-call(s32[1]{0:T(128)S(6)} %copy.14.count, s32[1,96]{1,0:T(1,128)} %owner_at.1, s32[1,96]{1,0:T(1,128)} %block_at.1, s32[1,192]{1,0:T(1,128)} %target_at.1, s32[1,192]{1,0:T(1,128)} %source_at.1, f32[1,128]{1,0:T(1,128)} %bitcast.6, f32[1,128]{1,0:T(1,128)} %bitcast.7, ...), custom_call_target="tpu_custom_call" | custom-call | flops 4294967296 | bytes 33554432 | tf_op jit(solution)/shard_map/exchange/pallas_call | solution.py:498
  165.0 2.4 %finish.1 = (bf16[32,128,128]{2,1,0:T(8,128)(2,1)}, bf16[32,128,128]{2,1,0:T(8,128)(2,1)}) custom-call(bf16[32,128,128]{2,1,0:T(8,128)(2,1)} %get-tuple-element.6.hidden_at, bf16[32,128,128]{2,1,0:T(8,128)(2,1)} %get-tuple-element.7.embedding_at), custom_call_target="tpu_custom_call" | custom-call | bytes 4194304 | tf_op jit(solution)/shard_map/finish/pallas_call | solution.py:578

commit v7 on v6

--- a/solution.py
+++ b/solution.py
@@ -14,6 +14,7 @@
 SHARE = 16
 PAIRS = (TILES + NB) // 2
 UNROLL = 8
+EARLY = (4, 5)
 FIRSTS = (4, 2, 6, 0)
 MESH = pl.DeviceIdType.MESH
 
@@ -95,7 +96,7 @@
     kept[1:2, 0:128] = jnp.where(many > 0, 1.0, 0.0)
 
 
-COPIES = 106
+COPIES = 108
 
 
 def exchange_kernel(
@@ -141,6 +142,8 @@
     down_past,
     up_past_two,
     down_past_two,
+    early_out,
+    early_in,
     relay_out,
     relay_in,
     share,
@@ -331,6 +334,24 @@
         share[at + 14] = relay_in[layer, 2, g]
         share[at + 15] = relay_in[layer, 3, g]
 
+    def send_early():
+        for side, (table, sign) in enumerate(((up_past, 1), (down_past, -1))):
+            for g in EARLY:
+                for slot in range(2):
+                    early_out[side, (g - EARLY[0]) * 2 + slot] = table[pick(sign, g, -sign, slot)]
+        return [
+            send(early_out.at[0], early_in.at[0], at_z(1)),
+            send(early_out.at[1], early_in.at[1], at_z(-1)),
+        ]
+
+    def forward_early(copies):
+        arrived(copies)
+        for g in EARLY:
+            for slot in range(2):
+                share[g * SHARE + 6 + slot] = early_in[0, (g - EARLY[0]) * 2 + slot]
+                share[g * SHARE + 8 + slot] = early_in[1, (g - EARLY[0]) * 2 + slot]
+        return [send_share(g, 6, 4, sources_two) for g in EARLY]
+
     def forward_far(layer, relays, sources, between):
         copies = []
         for first, then in zip(FIRSTS, between):
@@ -405,13 +426,13 @@
     hop = []
     for i in range(2):
         arrived(past[2 * i] + past[2 * i + 1])
+        if i == 1:
+            early = send_early()
         hop.append(along_both(up_past, down_past, up_past_two, down_past_two, halves[i]))
     keep_own(sources_one, 3)
     arrived(halo_copies)
     for copy in halo_copies:
         copy.wait_send()
-    pack_share([(0, table_past), (1, up_past), (2, down_past)])
-    last_copies = [send_share(g, 0, 6, sources_two) for g in others]
     to_near.wait()
     to_sources.wait()
     multiply(sources_one)
@@ -428,24 +449,29 @@
     from_below.append(send(hidden.at[high], near_y.at[0, high], at_y(1)))
     from_above.append(send(hidden.at[low], near_y.at[1, low], at_y(-1)))
 
+    pack_share([(0, table_past), (1, up_past), (2, down_past)])
+    last_copies = [send_share(g, 0, 6, sources_two) for g in others]
+    last_copies += forward_early(early)
     for copies in relays.values():
         for copy in copies:
             copy.wait_send()
+    arrived([from_below[0], from_above[0]])
+    across = [
+        send(near_y.at[0, low], far_y.at[low], at_y(1)),
+        send(near_y.at[1, high], far_y.at[high], at_y(-1)),
+    ]
     for copies in hop:
         arrived(copies)
     relays_two = {}
     for first in FIRSTS:
         pack_relay(up_past_two, down_past_two, first)
         relays_two[first] = send_relay(1, first)
+        if first == EARLY[0]:
+            continue
         pack_share([(3, up_past_two), (4, down_past_two)], first)
         for g in (first, first + 1):
             if g > 0:
                 last_copies.append(send_share(g, 6, 4, sources_two))
-    arrived([from_below[0], from_above[0]])
-    across = [
-        send(near_y.at[0, low], far_y.at[low], at_y(1)),
-        send(near_y.at[1, high], far_y.at[high], at_y(-1)),
-    ]
 
     def part(shift):
         return weight[pl.ds(pl.multiple_of(lax.rem(y + shift, NY) * BLOCK, BLOCK), BLOCK), :]
@@ -520,6 +546,8 @@
             pltpu.SMEM((5, GROUPS, 8, 128), jnp.int32),
             pltpu.VMEM((2, NB * BLOCK // 4, 4 * BLOCK), jnp.bfloat16),
             *[blocks(NB)] * 10,
+            blocks(2, 4),
+            blocks(2, 4),
             blocks(4, 2 * GROUPS),
             blocks(2, 4, 2 * GROUPS),
             blocks(GROUPS * SHARE),

time: 168 us -> 170 us (1.012)
  Pallas kernels: 166 us -> 169 us
    pallas_call x1, Pallas kernels: 164 us -> 166 us  [exchange(): pl.pallas_call(exchange_kernel, out_shape=(jax.ShapeDtypeStruct((NB, BLOC...]
where the time goes in v7:
time: 170 us
  Pallas kernels  169 us (99%)
    pallas_call x1, Pallas kernels, exchange(): pl.pallas_call(exchange_kernel, out_shape=(jax.ShapeDtypeStruct((NB, BLOC...  166 us

profile of v7, /device:TPU:1, one launch (start us, length us, event | category | flops | bytes accessed | tf_op | source)
XLA Modules:
  0.0 170.2 jit_solution(3202120106169594731)
XLA Ops:
  1.3 166.5 %exchange.1 = (bf16[32,128,128]{2,1,0:T(8,128)(2,1)}, bf16[32,128,128]{2,1,0:T(8,128)(2,1)}) custom-call(s32[1]{0:T(128)S(6)} %copy.14.count, s32[1,96]{1,0:T(1,128)} %owner_at.1, s32[1,96]{1,0:T(1,128)} %block_at.1, s32[1,192]{1,0:T(1,128)} %target_at.1, s32[1,192]{1,0:T(1,128)} %source_at.1, f32[1,128]{1,0:T(1,128)} %bitcast.6, f32[1,128]{1,0:T(1,128)} %bitcast.7, ...), custom_call_target="tpu_custom_call" | custom-call | flops 4294967296 | bytes 33554432 | tf_op jit(solution)/shard_map/exchange/pallas_call | solution.py:524
  167.8 2.4 %finish.1 = (bf16[32,128,128]{2,1,0:T(8,128)(2,1)}, bf16[32,128,128]{2,1,0:T(8,128)(2,1)}) custom-call(bf16[32,128,128]{2,1,0:T(8,128)(2,1)} %get-tuple-element.6.hidden_at, bf16[32,128,128]{2,1,0:T(8,128)(2,1)} %get-tuple-element.7.embedding_at), custom_call_target="tpu_custom_call" | custom-call | bytes 4194304 | tf_op jit(solution)/shard_map/finish/pallas_call | solution.py:606

commit v8 on v6

--- a/solution.py
+++ b/solution.py
@@ -95,7 +95,7 @@
     kept[1:2, 0:128] = jnp.where(many > 0, 1.0, 0.0)
 
 
-COPIES = 106
+COPIES = 71
 
 
 def exchange_kernel(
@@ -231,9 +231,9 @@
 
     started = []
 
-    def send(src, dst, device):
-        i = used[0]
-        used[0] += 1
+    def send(src, dst, device, shared=None):
+        i = used[0] if shared is None else shared
+        used[0] += shared is None
         copy = pltpu.make_async_remote_copy(
             src_ref=src,
             dst_ref=dst,
@@ -243,7 +243,8 @@
             device_id_type=MESH,
         )
         copy.start()
-        started.append(copy)
+        if shared is None:
+            started.append(copy)
         return copy
 
     def arrived(copies):
@@ -304,7 +305,19 @@
 
     def send_share(g, start, size, sources):
         at = g * SHARE + start
-        return send(share.at[pl.ds(at, size)], sources.at[pl.ds(NB + at, size)], at_slab(g))
+        layer = 0 if sources is sources_one else 1
+        send(share.at[pl.ds(at, size)], sources.at[pl.ds(NB + at, size)], at_slab(g), COPIES + layer)
+
+    def shares(layer, sources):
+        rest = (GROUPS - 1) * SHARE
+        return pltpu.make_async_remote_copy(
+            src_ref=share.at[pl.ds(SHARE, rest)],
+            dst_ref=sources.at[pl.ds(NB + SHARE, rest)],
+            send_sem=send_sem.at[COPIES + layer],
+            recv_sem=recv_sem.at[COPIES + layer],
+            device_id=at_slab(1),
+            device_id_type=MESH,
+        )
 
     def pack_relay(up, down, first):
         @pl.loop(first, first + 2)
@@ -332,15 +345,13 @@
         share[at + 15] = relay_in[layer, 3, g]
 
     def forward_far(layer, relays, sources, between):
-        copies = []
         for first, then in zip(FIRSTS, between):
             arrived(relays[first])
             for g in (first, first + 1):
                 pack_far(layer, g)
                 if g > 0:
-                    copies.append(send_share(g, 10, 6, sources))
+                    send_share(g, 10, 6, sources)
             then()
-        return copies
 
     def keep_own(sources, i):
         copy = pltpu.make_async_copy(
@@ -393,13 +404,14 @@
         pack_relay(up_two, down_two, first)
         relays[first] = send_relay(0, first)
     pack_share([(3, up_two), (4, down_two)])
-    halo_copies = [send_share(g, 0, 10, sources_one) for g in others]
+    for g in others:
+        send_share(g, 0, 10, sources_one)
 
     def start_two():
         start_past()
         start_past()
 
-    halo_copies += forward_far(
+    forward_far(
         0, relays, sources_one, (nothing, start_past, start_two, nothing)
     )
     hop = []
@@ -407,11 +419,11 @@
         arrived(past[2 * i] + past[2 * i + 1])
         hop.append(along_both(up_past, down_past, up_past_two, down_past_two, halves[i]))
     keep_own(sources_one, 3)
-    arrived(halo_copies)
-    for copy in halo_copies:
-        copy.wait_send()
+    shares(0, sources_one).wait_recv()
+    shares(0, sources_one).wait_send()
     pack_share([(0, table_past), (1, up_past), (2, down_past)])
-    last_copies = [send_share(g, 0, 6, sources_two) for g in others]
+    for g in others:
+        send_share(g, 0, 6, sources_two)
     to_near.wait()
     to_sources.wait()
     multiply(sources_one)
@@ -431,6 +443,11 @@
     for copies in relays.values():
         for copy in copies:
             copy.wait_send()
+    arrived([from_below[0], from_above[0]])
+    across = [
+        send(near_y.at[0, low], far_y.at[low], at_y(1)),
+        send(near_y.at[1, high], far_y.at[high], at_y(-1)),
+    ]
     for copies in hop:
         arrived(copies)
     relays_two = {}
@@ -440,12 +457,7 @@
         pack_share([(3, up_past_two), (4, down_past_two)], first)
         for g in (first, first + 1):
             if g > 0:
-                last_copies.append(send_share(g, 6, 4, sources_two))
-    arrived([from_below[0], from_above[0]])
-    across = [
-        send(near_y.at[0, low], far_y.at[low], at_y(1)),
-        send(near_y.at[1, high], far_y.at[high], at_y(-1)),
-    ]
+                send_share(g, 6, 4, sources_two)
 
     def part(shift):
         return weight[pl.ds(pl.multiple_of(lax.rem(y + shift, NY) * BLOCK, BLOCK), BLOCK), :]
@@ -465,9 +477,9 @@
                 )
             sources_two[here] = total.astype(jnp.bfloat16).reshape(4, BLOCK, BLOCK)
 
-    last_copies += forward_far(1, relays_two, sources_two, (nothing, nothing, project_hidden, nothing))
+    forward_far(1, relays_two, sources_two, (nothing, nothing, project_hidden, nothing))
     keep_own(sources_two, 4)
-    arrived(last_copies)
+    shares(1, sources_two).wait_recv()
     multiply(sources_two)
 
     outs = []
@@ -485,7 +497,8 @@
     for copy in outs:
         copy.wait()
     assert used[0] == COPIES
-    waited = halo_copies + [c for copies in relays.values() for c in copies]
+    shares(1, sources_two).wait_send()
+    waited = [c for copies in relays.values() for c in copies]
     for copy in started:
         if not any(copy is w for w in waited):
             copy.wait_send()
@@ -529,8 +542,8 @@
             pltpu.VMEM((PAIRS, BLOCK, BLOCK), jnp.float32),
             blocks(2, NB),
             blocks(NB),
-            pltpu.SemaphoreType.DMA((COPIES,)),
-            pltpu.SemaphoreType.DMA((COPIES,)),
+            pltpu.SemaphoreType.DMA((COPIES + 2,)),
+            pltpu.SemaphoreType.DMA((COPIES + 2,)),
             pltpu.SemaphoreType.DMA((28,)),
         ],
         compiler_params=pltpu.CompilerParams(

time: 168 us -> 168 us (level)
  no operation moved by 1% of the time
where the time goes in v8:
time: 168 us
  Pallas kernels  166 us (99%)
    pallas_call x1, Pallas kernels, exchange(): pl.pallas_call(exchange_kernel, out_shape=(jax.ShapeDtypeStruct((NB, BLOC...  164 us

profile of v8, /device:TPU:1, one launch (start us, length us, event | category | flops | bytes accessed | tf_op | source)
XLA Modules:
  0.0 167.8 jit_solution(7437891208746558386)
XLA Ops:
  1.3 164.1 %exchange.1 = (bf16[32,128,128]{2,1,0:T(8,128)(2,1)}, bf16[32,128,128]{2,1,0:T(8,128)(2,1)}) custom-call(s32[1]{0:T(128)S(6)} %copy.14.count, s32[1,96]{1,0:T(1,128)} %owner_at.1, s32[1,96]{1,0:T(1,128)} %block_at.1, s32[1,192]{1,0:T(1,128)} %target_at.1, s32[1,192]{1,0:T(1,128)} %source_at.1, f32[1,128]{1,0:T(1,128)} %bitcast.6, f32[1,128]{1,0:T(1,128)} %bitcast.7, ...), custom_call_target="tpu_custom_call" | custom-call | flops 4294967296 | bytes 33554432 | tf_op jit(solution)/shard_map/exchange/pallas_call | solution.py:511
  165.4 2.4 %finish.1 = (bf16[32,128,128]{2,1,0:T(8,128)(2,1)}, bf16[32,128,128]{2,1,0:T(8,128)(2,1)}) custom-call(bf16[32,128,128]{2,1,0:T(8,128)(2,1)} %get-tuple-element.6.hidden_at, bf16[32,128,128]{2,1,0:T(8,128)(2,1)} %get-tuple-element.7.embedding_at), custom_call_target="tpu_custom_call" | custom-call | bytes 4194304 | tf_op jit(solution)/shard_map/finish/pallas_call | solution.py:591
